TPU v7x, 128 devices: a whole 4x4x4 slice. The times are simulated.
128 devices in a mesh: lon: 16 (over z, x_hi, core), lat: 8 (over x_lo, y).
Axes of the slice: x: 4 (x_hi: 2, x_lo: 2; x = x_hi * 2 + x_lo), y: 4, z: 4, core: 2. Of those that a mesh axis runs over, the one named last changes fastest.
Arguments:
- adjoint_end: float32 [4, 32, 32, 2048], P(None, None, 'lat', 'lon'), may hold values from -6 to 6
- face_courant: bfloat16 [4, 4, 32, 32, 2048], P(None, None, None, 'lat', 'lon'), may hold values from 0.019897461 to 0.22949219
- mixing: bfloat16 [31, 32, 2048], P(None, 'lat', 'lon'), may hold values from 0.019897461 to 0.19921875
- row_shift: int32 [4, 32], P(None, 'lat'), may hold values from 0 to 2047, as said below
- tile_jac: float32 [128, 4, 128, 8, 128], P(('lon', 'lat')), may hold values from -6 to 6
- tile_cell: int32 [128, 4, 128, 8], P(('lon', 'lat')), may hold values from 0 to 511
- tile_count: int32 [128, 4, 128], P(('lon', 'lat')), may hold values from 1 to 8, as said below
Outputs:
- adjoint_start: float32 [4, 32, 32, 2048], P(None, None, 'lat', 'lon')
- flux_sensitivity: float32 [4, 32, 2048], P(None, 'lat', 'lon')
Inputs may be any that keep to these rules, and one draw needn't show every extreme that they name: `row_shift`: row j's shift is below max(2048 // (1 + min(j, 31 - j)), 2) at every step and equals that bound minus one at some step; the first row's shift is 2047 at every step. `tile_cell`: cell index row * 128 + column within the owner's block. `tile_count`: slots 0 to count - 1 of a tile hold soundings; the rest are padding. At every step some owner receives 8 soundings from every device.
All inputs are finite; a program needn't handle non-finite values.
Results may differ from a plain program's by a relative error of at most 0.0003.
Values sent between devices are 32-bit elements; how exact they have to be, the bound alone decides.
A program may use at most 128 MiB of HBM per device.

v0:
```python
import jax
import jax.numpy as jnp
from jax import lax
from jax.sharding import PartitionSpec as P


def with_halo(block, sides, width, periodic):
    for axis, dim in sides:
        count = lax.axis_size(axis)
        forward = [(i, i + 1) for i in range(count - 1)]
        if periodic:
            forward.append((count - 1, 0))
        backward = [(target, source) for source, target in forward]
        low = lax.ppermute(
            lax.slice_in_dim(block, block.shape[dim] - width, None, axis=dim), axis, forward
        )
        high = lax.ppermute(lax.slice_in_dim(block, 0, width, axis=dim), axis, backward)
        block = jnp.concatenate([low, block, high], axis=dim)
    return block


def local_forcing(jac_step, cell_step, count_step, tracers, levels, lat_rows, lon_cells):
    slot_ids = jnp.arange(jac_step.shape[1], dtype=jnp.int32)
    live = (slot_ids[None, :] < count_step[:, None]).astype(jnp.float32)
    values = (jac_step * live[..., None]).reshape(-1, jac_step.shape[2])
    cell_ids = jnp.arange(lat_rows * lon_cells, dtype=jnp.int32)
    onehot = (cell_step.reshape(-1)[:, None] == cell_ids[None, :]).astype(jnp.float32)
    total = lax.dot_general(
        values,
        onehot,
        (((0,), (0,)), ((), ())),
        precision=lax.Precision.HIGHEST,
        preferred_element_type=jnp.float32,
    )
    return total.reshape(tracers, levels, lat_rows, lon_cells)


def mix_levels(summed, mixing):
    rates = mixing.astype(jnp.float32)[None]
    fluxes = rates * (summed[:, 1:] - summed[:, :-1])
    zero_layer = jnp.zeros_like(summed[:, :1])
    return (
        summed
        + jnp.concatenate([fluxes, zero_layer], axis=1)
        - jnp.concatenate([zero_layer, fluxes], axis=1)
    )


def slice_rows(source_rows, offsets, width):

    def take_row(row_block, offset):
        return lax.dynamic_slice_in_dim(row_block, offset, width, axis=2)

    return jax.vmap(take_row, in_axes=(2, 0), out_axes=2)(source_rows, offsets)


def roll_rows(mixed, shifts):
    lon_cells = mixed.shape[3]
    whole_cycle = lax.all_gather(mixed, "lon", axis=3, tiled=True)
    cycle_cells = whole_cycle.shape[3]
    start = lax.axis_index("lon") * lon_cells
    extended = jnp.concatenate([whole_cycle, whole_cycle[:, :, :, :lon_cells]], axis=3)
    offsets = (start + shifts) % cycle_cells
    return slice_rows(extended, offsets, lon_cells)


def transport(rolled, courant):
    to_north = courant[0].astype(jnp.float32)
    to_south = courant[1].astype(jnp.float32)
    to_east = courant[2].astype(jnp.float32)
    to_west = courant[3].astype(jnp.float32)
    lat_padded = with_halo(rolled, (("lat", 2),), 1, False)
    lon_padded = with_halo(rolled, (("lon", 3),), 1, True)
    above_row = lat_padded[:, :, 2:]
    below_row = lat_padded[:, :, :-2]
    east_cell = lon_padded[:, :, :, 2:]
    west_cell = lon_padded[:, :, :, :-2]
    return (
        rolled
        + to_north * (above_row - rolled)
        + to_south * (below_row - rolled)
        + to_east * (east_cell - rolled)
        + to_west * (west_cell - rolled)
    )


def shards(adjoint_end, face_courant, mixing, row_shift, tile_jac, tile_cell, tile_count):
    tracers, levels, lat_rows, lon_cells = adjoint_end.shape
    steps = tile_jac.shape[1]
    got_jac, got_cell, got_count = (
        lax.all_to_all(tile_jac, ("lon", "lat"), split_axis=2, concat_axis=0, tiled=True),
        lax.all_to_all(tile_cell, ("lon", "lat"), split_axis=2, concat_axis=0, tiled=True),
        lax.all_to_all(tile_count, ("lon", "lat"), split_axis=2, concat_axis=0, tiled=True),
    )
    got_jac = got_jac.reshape((got_jac.shape[0], steps) + got_jac.shape[3:])
    got_cell = got_cell.reshape((got_cell.shape[0], steps) + got_cell.shape[3:])
    got_count = got_count.reshape((got_count.shape[0], steps))
    adjoint = adjoint_end
    flux_sensitivity = jnp.zeros((tracers, lat_rows, lon_cells), jnp.float32)
    for time_step in range(steps - 1, -1, -1):
        forcing = local_forcing(
            got_jac[:, time_step],
            got_cell[:, time_step],
            got_count[:, time_step],
            tracers,
            levels,
            lat_rows,
            lon_cells,
        )
        summed = adjoint + forcing
        mixed = mix_levels(summed, mixing)
        rolled = roll_rows(mixed, row_shift[time_step])
        adjoint = transport(rolled, face_courant[:, time_step])
        flux_sensitivity = flux_sensitivity + adjoint[:, 0]
    return (adjoint, flux_sensitivity)


def solution(mesh):
    in_specs = (
        P(None, None, "lat", "lon"),
        P(None, None, None, "lat", "lon"),
        P(None, "lat", "lon"),
        P(None, "lat"),
        P(("lon", "lat"), None, None, None, None),
        P(("lon", "lat"), None, None, None),
        P(("lon", "lat"), None, None),
    )
    out_specs = (P(None, None, "lat", "lon"), P(None, "lat", "lon"))
    return jax.shard_map(shards, mesh=mesh, in_specs=in_specs, out_specs=out_specs, check_vma=False)
```

profile of v0, /device:TPU:3, one launch (start us, length us, event | category | flops | bytes accessed | tf_op | source)
XLA Modules:
  0.0 505.7 jit_solution(9470553493311217429)
XLA Ops:
  8.6 10.8 %all-to-all-start.1 = ((s32[1,4,128]{1,0,2:T(1,128)}), s32[1,4,128]{1,0,2:T(1,128)S(1)}, u32[]{:S(2)}, u32[]{:S(2)}) async-start(s32[1,4,128]{1,0,2:T(1,128)} %copy.110), calls=%async_computation.1 | async-start | bytes 131072 | tf_op jit(solution)/shard_map/all_to_all | solution.py:93
  21.0 7.2 %all-to-all-done.1 = s32[1,4,128]{1,0,2:T(1,128)S(1)} async-done(((s32[1,4,128]{1,0,2:T(1,128)}), s32[1,4,128]{1,0,2:T(1,128)S(1)}, u32[]{:S(2)}, u32[]{:S(2)}) %all-to-all-start.1) | async-done | bytes 2080 | tf_op jit(solution)/shard_map/all_to_all | solution.py:93
  28.2 5.3 %all-to-all-start.2 = ((s32[1,4,128,8]{3,1,0,2:T(4,128)}), s32[1,4,128,8]{3,1,0,2:T(4,128)S(1)}, u32[]{:S(2)}, u32[]{:S(2)}) async-start(s32[1,4,128,8]{3,1,0,2:T(4,128)} %copy.112), calls=%async_computation.2 | async-start | bytes 524288 | tf_op jit(solution)/shard_map/all_to_all | solution.py:92
  36.7 6.9 %all-to-all-done.2 = s32[1,4,128,8]{3,1,0,2:T(4,128)S(1)} async-done(((s32[1,4,128,8]{3,1,0,2:T(4,128)}), s32[1,4,128,8]{3,1,0,2:T(4,128)S(1)}, u32[]{:S(2)}, u32[]{:S(2)}) %all-to-all-start.2) | async-done | bytes 16416 | tf_op jit(solution)/shard_map/all_to_all | solution.py:92
  51.1 26.1 %all-to-all-done = f32[1,4,128,8,128]{4,3,1,0,2:T(8,128)S(1)} async-done(((f32[1,4,128,8,128]{4,3,1,0,2:T(8,128)}), f32[1,4,128,8,128]{4,3,1,0,2:T(8,128)S(1)}, u32[]{:S(2)}, u32[]{:S(2)}) %all-to-all-start) | async-done | bytes 2097184 | tf_op jit(solution)/shard_map/all_to_all | solution.py:91
  82.7 53.6 %all-gather.5.cloned.1.call-done = f32[4,32,4,2048]{3,1,2,0:T(8,128)} async-done(((f32[4,32,4,128]{3,1,2,0:T(8,128)}), f32[4,32,4,2048]{3,1,2,0:T(8,128)}) %all-gather.5.cloned.1.call-update) | async-done | bytes 4194320 | tf_op jit(solution)/shard_map/all_gather | solution.py:59
  142.0 15.1 %copy.115 = f32[4,4,32,2176]{2,1,0,3:T(4,128)} copy(f32[4,4,32,2176]{3,2,0,1:T(8,128)} %maximum_bitcast_fusion) | data formatting | bytes 8912896 | tf_op jit(solution)/shard_map/vmap()/transpose | solution.py:52
  157.1 8.3 %gather_fusion = f32[4,4,32,128]{2,1,3,0:T(4,128)} fusion(f32[4,4,32,2176]{2,1,0,3:T(4,128)} %copy.115, s32[4]{0:T(128)S(1)} %get-tuple-element.56), kind=kCustom, calls=%fused_computation | custom fusion | bytes 524352 | tf_op jit(solution)/shard_map/vmap()/gather | solution.py:52
  171.7 5.3 %collective-permute-start = (f32[4,32,1,128]{3,1,2,0:T(8,128)}, f32[4,32,1,128]{3,1,2,0:T(8,128)S(1)}, u32[]{:S(2)}, u32[]{:S(2)}) collective-permute-start(f32[4,32,1,128]{3,1,2,0:T(8,128)} %get-tuple-element.50), channel_id=1, source_target_pairs={{1,0},{2,1},{3,2},{4,3},{5,4},{6,5},{7,6},{9,8},{10,9},{11,10},{12... | collective-permute-start | bytes 196616 | tf_op jit(solution)/shard_map/ppermute | solution.py:17
  187.7 52.1 %all-gather.7.cloned.1.call-done = f32[4,32,4,2048]{3,1,2,0:T(8,128)} async-done(((f32[4,32,4,128]{3,1,2,0:T(8,128)}), f32[4,32,4,2048]{3,1,2,0:T(8,128)}) %all-gather.7.cloned.1.call-update) | async-done | bytes 4194320 | tf_op jit(solution)/shard_map/all_gather | solution.py:59
  245.4 15.1 %copy.122 = f32[4,4,32,2176]{2,1,0,3:T(4,128)} copy(f32[4,4,32,2176]{3,2,0,1:T(8,128)} %maximum_bitcast_fusion.1) | data formatting | bytes 8912896 | tf_op jit(solution)/shard_map/vmap()/transpose | solution.py:52
  260.5 7.4 %gather_fusion.1 = f32[4,4,32,128]{2,1,3,0:T(4,128)S(1)} fusion(f32[4,4,32,2176]{2,1,0,3:T(4,128)} %copy.122, s32[4]{0:T(128)S(1)} %copy-done.10), kind=kCustom, calls=%fused_computation.1 | custom fusion | bytes 524352 | tf_op jit(solution)/shard_map/vmap()/gather | solution.py:52
  268.9 5.3 %collective-permute-start.4 = (f32[4,32,1,128]{3,1,2,0:T(8,128)}, f32[4,32,1,128]{3,1,2,0:T(8,128)S(1)}, u32[]{:S(2)}, u32[]{:S(2)}) collective-permute-start(f32[4,32,1,128]{3,1,2,0:T(8,128)} %get-tuple-element.46), channel_id=1, source_target_pairs={{1,0},{2,1},{3,2},{4,3},{5,4},{6,5},{7,6},{9,8},{10,9},{11,10},{12... | collective-permute-start | bytes 196616 | tf_op jit(solution)/shard_map/ppermute | solution.py:17
  281.4 5.9 %collective-permute-done.6 = f32[4,32,4,1]{3,1,2,0:T(8,128)S(1)} collective-permute-done((f32[4,32,4,1]{3,1,2,0:T(8,128)}, f32[4,32,4,1]{3,1,2,0:T(8,128)S(1)}, u32[]{:S(2)}, u32[]{:S(2)}) %collective-permute-start.6) | collective-permute-done | bytes 2080 | tf_op jit(solution)/shard_map/ppermute | solution.py:17
  291.4 54.6 %all-gather.9.cloned.1.call-done = f32[4,32,4,2048]{3,1,2,0:T(8,128)} async-done(((f32[4,32,4,128]{3,1,2,0:T(8,128)}), f32[4,32,4,2048]{3,1,2,0:T(8,128)}) %all-gather.9.cloned.1.call-update) | async-done | bytes 4194320 | tf_op jit(solution)/shard_map/all_gather | solution.py:59
  351.6 15.1 %copy.129 = f32[4,4,32,2176]{2,1,0,3:T(4,128)} copy(f32[4,4,32,2176]{3,2,0,1:T(8,128)} %maximum_bitcast_fusion.2) | data formatting | bytes 8912896 | tf_op jit(solution)/shard_map/vmap()/transpose | solution.py:52
  366.7 7.4 %gather_fusion.2 = f32[4,4,32,128]{2,1,3,0:T(4,128)S(1)} fusion(f32[4,4,32,2176]{2,1,0,3:T(4,128)} %copy.129, s32[4]{0:T(128)S(1)} %get-tuple-element.57), kind=kCustom, calls=%fused_computation.2 | custom fusion | bytes 524352 | tf_op jit(solution)/shard_map/vmap()/gather | solution.py:52
  375.1 5.3 %collective-permute-start.8 = (f32[4,32,1,128]{3,1,2,0:T(8,128)}, f32[4,32,1,128]{3,1,2,0:T(8,128)}, u32[]{:S(2)}, u32[]{:S(2)}) collective-permute-start(f32[4,32,1,128]{3,1,2,0:T(8,128)} %get-tuple-element.42), channel_id=1, source_target_pairs={{1,0},{2,1},{3,2},{4,3},{5,4},{6,5},{7,6},{9,8},{10,9},{11,10},{12... | collective-permute-start | bytes 196616 | tf_op jit(solution)/shard_map/ppermute | solution.py:17
  386.7 6.9 %collective-permute-done.10 = f32[4,32,4,1]{3,1,2,0:T(8,128)S(1)} collective-permute-done((f32[4,32,4,1]{3,1,2,0:T(8,128)}, f32[4,32,4,1]{3,1,2,0:T(8,128)S(1)}, u32[]{:S(2)}, u32[]{:S(2)}) %collective-permute-start.10) | collective-permute-done | bytes 2080 | tf_op jit(solution)/shard_map/ppermute | solution.py:17
  396.9 54.4 %all-gather.11.cloned.1.call-done = f32[4,32,4,2048]{3,1,2,0:T(8,128)} async-done(((f32[4,32,4,128]{3,1,2,0:T(8,128)}), f32[4,32,4,2048]{3,1,2,0:T(8,128)}) %all-gather.11.cloned.1.call-update) | async-done | bytes 4194320 | tf_op jit(solution)/shard_map/all_gather | solution.py:59
  457.0 15.1 %copy.136 = f32[4,4,32,2176]{2,1,0,3:T(4,128)} copy(f32[4,4,32,2176]{3,2,0,1:T(8,128)} %maximum_bitcast_fusion.3) | data formatting | bytes 8912896 | tf_op jit(solution)/shard_map/vmap()/transpose | solution.py:52
  472.1 7.4 %gather_fusion.3 = f32[4,4,32,128]{2,1,3,0:T(4,128)S(1)} fusion(f32[4,4,32,2176]{2,1,0,3:T(4,128)} %copy.136, s32[4]{0:T(128)S(1)} %get-tuple-element.54), kind=kCustom, calls=%fused_computation.3 | custom fusion | bytes 524352 | tf_op jit(solution)/shard_map/vmap()/gather | solution.py:52
  479.8 5.3 %collective-permute-start.12 = (f32[4,32,1,128]{3,1,2,0:T(8,128)S(1)}, f32[4,32,1,128]{3,1,2,0:T(8,128)S(1)}, u32[]{:S(2)}, u32[]{:S(2)}) collective-permute-start(f32[4,32,1,128]{3,1,2,0:T(8,128)S(1)} %get-tuple-element.38), channel_id=1, source_target_pairs={{1,0},{2,1},{3,2},{4,3},{5,4},{6,5},{7,6},{9,8},{10,9},{11,10},{12... | collective-permute-start | bytes 196616 | tf_op jit(solution)/shard_map/ppermute | solution.py:17
  490.5 6.8 %collective-permute-done.14 = f32[4,32,4,1]{3,1,2,0:T(8,128)S(1)} collective-permute-done((f32[4,32,4,1]{3,1,2,0:T(8,128)S(1)}, f32[4,32,4,1]{3,1,2,0:T(8,128)S(1)}, u32[]{:S(2)}, u32[]{:S(2)}) %collective-permute-start.14) | collective-permute-done | bytes 2080 | tf_op jit(solution)/shard_map/ppermute | solution.py:17
  (138 shorter events, 88.7 us)
Async XLA Ops:
  8.6 19.6 %all-to-all-start.1 = ((s32[1,4,128]{1,0,2:T(1,128)}), s32[1,4,128]{1,0,2:T(1,128)S(1)}, u32[]{:S(2)}, u32[]{:S(2)}) async-start(s32[1,4,128]{1,0,2:T(1,128)} %copy.110), calls=%async_computation.1 | async-start | bytes 131072 | tf_op jit(solution)/shard_map/all_to_all | solution.py:93
  28.2 15.4 %all-to-all-start.2 = ((s32[1,4,128,8]{3,1,0,2:T(4,128)}), s32[1,4,128,8]{3,1,0,2:T(4,128)S(1)}, u32[]{:S(2)}, u32[]{:S(2)}) async-start(s32[1,4,128,8]{3,1,0,2:T(4,128)} %copy.112), calls=%async_computation.2 | async-start | bytes 524288 | tf_op jit(solution)/shard_map/all_to_all | solution.py:92
  36.7 43.3 %copy-start.12 = (f32[4,32,4,128]{3,2,1,0:T(4,128)S(1)}, f32[4,32,4,128]{3,2,1,0:T(4,128)}, u32[]{:S(2)}) copy-start(f32[4,32,4,128]{3,2,1,0:T(4,128)} %param.7) | copy-start | bytes 786436
  43.6 33.6 %all-to-all-start = ((f32[1,4,128,8,128]{4,3,1,0,2:T(8,128)}), f32[1,4,128,8,128]{4,3,1,0,2:T(8,128)S(1)}, u32[]{:S(2)}, u32[]{:S(2)}) async-start(f32[1,4,128,8,128]{4,3,1,0,2:T(8,128)} %copy.109), calls=%async_computation | async-start | bytes 4194304 | tf_op jit(solution)/shard_map/all_to_all | solution.py:91
  48.8 87.5 %all-gather.5.cloned.1.call-start = ((), (), s32[]{:S(2)}) async-start(), calls=%async_computation.3 | async-start | bytes 4456448 | tf_op jit(solution)/shard_map/all_gather | solution.py:59
  82.1 157.7 %all-gather.7.cloned.1.call-start = ((), (), s32[]{:S(2)}) async-start(), calls=%async_computation.4 | async-start | bytes 4456448 | tf_op jit(solution)/shard_map/all_gather | solution.py:59
  168.5 11.6 %collective-permute-start.2 = (f32[4,32,4,1]{3,1,2,0:T(8,128)}, f32[4,32,4,1]{3,1,2,0:T(8,128)}, u32[]{:S(2)}, u32[]{:S(2)}) collective-permute-start(f32[4,32,4,1]{3,1,2,0:T(8,128)} %get-tuple-element.52), channel_id=1, source_target_pairs={{8,0},{16,8},{24,16},{32,24},{40,32},{48,40},{56,48},{64,56},{72,6... | collective-permute-start | bytes 6152 | tf_op jit(solution)/shard_map/ppermute | solution.py:17
  168.7 11.3 %collective-permute-start.3 = (f32[4,32,4,1]{3,1,2,0:T(8,128)}, f32[4,32,4,1]{3,1,2,0:T(8,128)}, u32[]{:S(2)}, u32[]{:S(2)}) collective-permute-start(f32[4,32,4,1]{3,1,2,0:T(8,128)} %get-tuple-element.53), channel_id=1, source_target_pairs={{0,8},{8,16},{16,24},{24,32},{32,40},{40,48},{48,56},{56,64},{64,7... | collective-permute-start | bytes 6152 | tf_op jit(solution)/shard_map/ppermute | solution.py:14
  171.7 8.3 %collective-permute-start = (f32[4,32,1,128]{3,1,2,0:T(8,128)}, f32[4,32,1,128]{3,1,2,0:T(8,128)S(1)}, u32[]{:S(2)}, u32[]{:S(2)}) collective-permute-start(f32[4,32,1,128]{3,1,2,0:T(8,128)} %get-tuple-element.50), channel_id=1, source_target_pairs={{1,0},{2,1},{3,2},{4,3},{5,4},{6,5},{7,6},{9,8},{10,9},{11,10},{12... | collective-permute-start | bytes 196616 | tf_op jit(solution)/shard_map/ppermute | solution.py:17
  177.0 7.2 %collective-permute-start.1 = (f32[4,32,1,128]{3,1,2,0:T(8,128)S(1)}, f32[4,32,1,128]{3,1,2,0:T(8,128)}, u32[]{:S(2)}, u32[]{:S(2)}) collective-permute-start(f32[4,32,1,128]{3,1,2,0:T(8,128)S(1)} %get-tuple-element.51), channel_id=1, source_target_pairs={{0,1},{1,2},{2,3},{3,4},{4,5},{5,6},{6,7},{8,9},{9,10},{10,11},{11... | collective-permute-start | bytes 196616 | tf_op jit(solution)/shard_map/ppermute | solution.py:14
  187.6 158.3 %all-gather.9.cloned.1.call-start = ((), (), s32[]{:S(2)}) async-start(), calls=%async_computation.5 | async-start | bytes 4456448 | tf_op jit(solution)/shard_map/all_gather | solution.py:59
  268.9 18.4 %collective-permute-start.4 = (f32[4,32,1,128]{3,1,2,0:T(8,128)}, f32[4,32,1,128]{3,1,2,0:T(8,128)S(1)}, u32[]{:S(2)}, u32[]{:S(2)}) collective-permute-start(f32[4,32,1,128]{3,1,2,0:T(8,128)} %get-tuple-element.46), channel_id=1, source_target_pairs={{1,0},{2,1},{3,2},{4,3},{5,4},{6,5},{7,6},{9,8},{10,9},{11,10},{12... | collective-permute-start | bytes 196616 | tf_op jit(solution)/shard_map/ppermute | solution.py:17
  274.1 13.8 %collective-permute-start.5 = (f32[4,32,1,128]{3,1,2,0:T(8,128)S(1)}, f32[4,32,1,128]{3,1,2,0:T(8,128)S(1)}, u32[]{:S(2)}, u32[]{:S(2)}) collective-permute-start(f32[4,32,1,128]{3,1,2,0:T(8,128)S(1)} %get-tuple-element.47), channel_id=1, source_target_pairs={{0,1},{1,2},{2,3},{3,4},{4,5},{5,6},{6,7},{8,9},{9,10},{10,11},{11... | collective-permute-start | bytes 196616 | tf_op jit(solution)/shard_map/ppermute | solution.py:14
  276.9 10.3 %collective-permute-start.6 = (f32[4,32,4,1]{3,1,2,0:T(8,128)}, f32[4,32,4,1]{3,1,2,0:T(8,128)S(1)}, u32[]{:S(2)}, u32[]{:S(2)}) collective-permute-start(f32[4,32,4,1]{3,1,2,0:T(8,128)} %get-tuple-element.48), channel_id=1, source_target_pairs={{8,0},{16,8},{24,16},{32,24},{40,32},{48,40},{56,48},{64,56},{72,6... | collective-permute-start | bytes 6152 | tf_op jit(solution)/shard_map/ppermute | solution.py:17
  277.5 9.8 %collective-permute-start.7 = (f32[4,32,4,1]{3,1,2,0:T(8,128)}, f32[4,32,4,1]{3,1,2,0:T(8,128)S(1)}, u32[]{:S(2)}, u32[]{:S(2)}) collective-permute-start(f32[4,32,4,1]{3,1,2,0:T(8,128)} %get-tuple-element.49), channel_id=1, source_target_pairs={{0,8},{8,16},{16,24},{24,32},{32,40},{40,48},{48,56},{56,64},{64,7... | collective-permute-start | bytes 6152 | tf_op jit(solution)/shard_map/ppermute | solution.py:14
  291.3 160.0 %all-gather.11.cloned.1.call-start = ((), (), s32[]{:S(2)}) async-start(), calls=%async_computation.6 | async-start | bytes 4456448 | tf_op jit(solution)/shard_map/all_gather | solution.py:59
  375.1 18.5 %collective-permute-start.8 = (f32[4,32,1,128]{3,1,2,0:T(8,128)}, f32[4,32,1,128]{3,1,2,0:T(8,128)}, u32[]{:S(2)}, u32[]{:S(2)}) collective-permute-start(f32[4,32,1,128]{3,1,2,0:T(8,128)} %get-tuple-element.42), channel_id=1, source_target_pairs={{1,0},{2,1},{3,2},{4,3},{5,4},{6,5},{7,6},{9,8},{10,9},{11,10},{12... | collective-permute-start | bytes 196616 | tf_op jit(solution)/shard_map/ppermute | solution.py:17
  380.4 13.3 %collective-permute-start.9 = (f32[4,32,1,128]{3,1,2,0:T(8,128)}, f32[4,32,1,128]{3,1,2,0:T(8,128)}, u32[]{:S(2)}, u32[]{:S(2)}) collective-permute-start(f32[4,32,1,128]{3,1,2,0:T(8,128)} %get-tuple-element.43), channel_id=1, source_target_pairs={{0,1},{1,2},{2,3},{3,4},{4,5},{5,6},{6,7},{8,9},{9,10},{10,11},{11... | collective-permute-start | bytes 196616 | tf_op jit(solution)/shard_map/ppermute | solution.py:14
  383.1 10.6 %collective-permute-start.10 = (f32[4,32,4,1]{3,1,2,0:T(8,128)}, f32[4,32,4,1]{3,1,2,0:T(8,128)S(1)}, u32[]{:S(2)}, u32[]{:S(2)}) collective-permute-start(f32[4,32,4,1]{3,1,2,0:T(8,128)} %get-tuple-element.44), channel_id=1, source_target_pairs={{8,0},{16,8},{24,16},{32,24},{40,32},{48,40},{56,48},{64,56},{72,6... | collective-permute-start | bytes 6152 | tf_op jit(solution)/shard_map/ppermute | solution.py:17
  383.6 10.0 %collective-permute-start.11 = (f32[4,32,4,1]{3,1,2,0:T(8,128)S(1)}, f32[4,32,4,1]{3,1,2,0:T(8,128)S(1)}, u32[]{:S(2)}, u32[]{:S(2)}) collective-permute-start(f32[4,32,4,1]{3,1,2,0:T(8,128)S(1)} %get-tuple-element.45), channel_id=1, source_target_pairs={{0,8},{8,16},{16,24},{24,32},{32,40},{40,48},{48,56},{56,64},{64,7... | collective-permute-start | bytes 6152 | tf_op jit(solution)/shard_map/ppermute | solution.py:14
  479.8 17.5 %collective-permute-start.12 = (f32[4,32,1,128]{3,1,2,0:T(8,128)S(1)}, f32[4,32,1,128]{3,1,2,0:T(8,128)S(1)}, u32[]{:S(2)}, u32[]{:S(2)}) collective-permute-start(f32[4,32,1,128]{3,1,2,0:T(8,128)S(1)} %get-tuple-element.38), channel_id=1, source_target_pairs={{1,0},{2,1},{3,2},{4,3},{5,4},{6,5},{7,6},{9,8},{10,9},{11,10},{12... | collective-permute-start | bytes 196616 | tf_op jit(solution)/shard_map/ppermute | solution.py:17
  485.0 12.3 %collective-permute-start.13 = (f32[4,32,1,128]{3,1,2,0:T(8,128)S(1)}, f32[4,32,1,128]{3,1,2,0:T(8,128)S(1)}, u32[]{:S(2)}, u32[]{:S(2)}) collective-permute-start(f32[4,32,1,128]{3,1,2,0:T(8,128)S(1)} %get-tuple-element.39), channel_id=1, source_target_pairs={{0,1},{1,2},{2,3},{3,4},{4,5},{5,6},{6,7},{8,9},{9,10},{10,11},{11... | collective-permute-start | bytes 196616 | tf_op jit(solution)/shard_map/ppermute | solution.py:14
  487.1 10.2 %collective-permute-start.14 = (f32[4,32,4,1]{3,1,2,0:T(8,128)S(1)}, f32[4,32,4,1]{3,1,2,0:T(8,128)S(1)}, u32[]{:S(2)}, u32[]{:S(2)}) collective-permute-start(f32[4,32,4,1]{3,1,2,0:T(8,128)S(1)} %get-tuple-element.40), channel_id=1, source_target_pairs={{8,0},{16,8},{24,16},{32,24},{40,32},{48,40},{56,48},{64,56},{72,6... | collective-permute-start | bytes 6152 | tf_op jit(solution)/shard_map/ppermute | solution.py:17
  487.7 9.6 %collective-permute-start.15 = (f32[4,32,4,1]{3,1,2,0:T(8,128)S(1)}, f32[4,32,4,1]{3,1,2,0:T(8,128)S(1)}, u32[]{:S(2)}, u32[]{:S(2)}) collective-permute-start(f32[4,32,4,1]{3,1,2,0:T(8,128)S(1)} %get-tuple-element.41), channel_id=1, source_target_pairs={{0,8},{8,16},{16,24},{24,32},{32,40},{40,48},{48,56},{56,64},{64,7... | collective-permute-start | bytes 6152 | tf_op jit(solution)/shard_map/ppermute | solution.py:14
  (12 other events, 298.3 us)
Sparse Core Ops, SparseCore 0:
  82.2 54.0 all-gather.4
  187.8 51.9 all-gather.6
  291.4 54.4 all-gather.8
  397.0 54.2 all-gather.10
where the time goes:
time: 509 us; the launch traced here: 506 us
  waiting for transfers between devices  278 us (55%)
  local copies, waits for them, and re-layouts  115 us (23%)
  starting transfers between devices  63.2 us (12%)
  other arithmetic  29.5 us (6%)
  between operations  14.3 us (3%)
    all_gather x4, waiting for transfers between devices, roll_rows(): whole_cycle = lax.all_gather(mixed, 'lon', axis=3, tiled=True)  215 us
    transpose x4, local copies, waits for them, and re-layouts, take_row(): return lax.dynamic_slice_in_dim(row_block, offset, width, axis=2)  60.5 us
    gather x8, local copies, waits for them, and re-layouts, take_row(): return lax.dynamic_slice_in_dim(row_block, offset, width, axis=2)  32.9 us
    all_to_all x1, waiting for transfers between devices, shards(): lax.all_to_all(tile_jac, ('lon', 'lat'), split_axis=2, concat_axis=0, til...  26.1 us
    ppermute x8, starting transfers between devices, with_halo(): lax.ppermute(lax.slice_in_dim(block, 0, width, axis=dim), axis, backward)  22.9 us
    ppermute x8, waiting for transfers between devices, with_halo(): lax.ppermute(lax.slice_in_dim(block, 0, width, axis=dim), axis, backward)  19.7 us
    ppermute x8, starting transfers between devices, with_halo(): lax.ppermute(lax.slice_in_dim(block, block.shape[dim] - width, None, axis...  18.8 us
    transpose x4, other arithmetic, take_row(): return lax.dynamic_slice_in_dim(row_block, offset, width, axis=2)  18.7 us
  transfers between devices with their start and end apart: 23, of which 11 were waited for; matrix products, arithmetic and copies ran while one was open for 2% of the time, Pallas kernels for 0%

commit v1 on v0

v1 whole, which is shorter than its diff:
```python
import functools

import jax
import jax.numpy as jnp
from jax import lax
from jax.experimental import pallas as pl
from jax.experimental.pallas import tpu as pltpu
from jax.sharding import PartitionSpec as P

MESH = pl.DeviceIdType.MESH
F32 = jnp.float32
N_LON = 16
N_LAT = 8
N_DEV = N_LON * N_LAT
SHIFT_LANE = 32


def lon_of_group(g):
    k = g // 2
    x_hi = k // 4
    z = k + x_hi * (7 - 2 * k)
    return z * 4 + x_hi * 2 + g % 2


def group_of_lon(lon):
    z = lon // 4
    k = z + (lon // 2) % 2 * (7 - 2 * z)
    return k * 2 + lon % 2


def remote(src, dst, send_sem, recv_sem, lon, lat):
    return pltpu.make_async_remote_copy(
        src_ref=src,
        dst_ref=dst,
        send_sem=send_sem,
        recv_sem=recv_sem,
        device_id=(lon, lat),
        device_id_type=MESH,
    )


def wait_bytes(ref, sem):
    pltpu.make_async_copy(ref, ref, sem).wait()


def kernel(
    adj, courant, mixing, jac, note,
    out, flux_out,
    jac_in, note_in, shifts, forcing, padded, rates, mixed, edges, courant_out,
    inbox, halo, courant_in, rates_in, rates_t, state, twice, rolled, final, final_out, flux, flux_send,
    js, jr, ns, nr, ps, pr, fs, fr, ks, kr, rs, rr, es, er, os, orv, xs, xr, sm,
):
    lon, lat = lax.axis_index("lon"), lax.axis_index("lat")
    me = lon * N_LAT + lat
    g = group_of_lon(lon)
    north, south = lax.rem(lat + N_LAT - 1, N_LAT), lax.rem(lat + 1, N_LAT)
    lon_up, lon_down = lon_of_group(lax.rem(g + 1, N_LON)), lon_of_group(lax.rem(g + N_LON - 1, N_LON))

    barrier = pltpu.get_barrier_semaphore()

    def peer(k):
        return lax.rem(lon + k // N_LAT, N_LON), lax.rem(lat + k % N_LAT, N_LAT)

    def greet(k, carry):
        pl.semaphore_signal(barrier, inc=1, device_id=peer(k), device_id_type=MESH)
        return carry

    lax.fori_loop(1, N_DEV, greet, 0)
    pl.semaphore_wait(barrier, N_DEV - 1)

    def send_tiles(t, notes):
        def body(k, carry):
            p_lon, p_lat = peer(k)
            owner = p_lon * N_LAT + p_lat
            if notes:
                remote(note.at[pl.ds(owner, 1)], note_in.at[pl.ds(me, 1)], ns, nr, p_lon, p_lat).start()
            remote(
                jac.at[t, pl.ds(owner * 8, 8)], jac_in.at[t, pl.ds(me * 8, 8)], js.at[t], jr.at[t], p_lon, p_lat
            ).start()
            return carry

        if notes:
            pltpu.make_async_copy(note.at[pl.ds(me, 1)], note_in.at[pl.ds(me, 1)], nr).start()
        pltpu.make_async_copy(jac.at[t, pl.ds(me * 8, 8)], jac_in.at[t, pl.ds(me * 8, 8)], jr.at[t]).start()
        lax.fori_loop(1, N_DEV, body, 0)

    def to_groups(send):
        def body(k, carry):
            target = lax.rem(lon + k, N_LON)
            send(group_of_lon(target), target)
            return carry

        lax.fori_loop(1, N_LON, body, 0)

    def send_blocks(src, dst, send_sem, recv_sem):
        pltpu.make_async_copy(src.at[pl.ds(g * 32, 32)], dst.at[pl.ds(lon * 32, 32)], recv_sem).start()

        def one(to, target):
            remote(
                src.at[pl.ds(to * 32, 32)], dst.at[pl.ds(lon * 32, 32)], send_sem, recv_sem, target, lat
            ).start()

        to_groups(one)

    def convert_courant(t):
        for face in range(4):
            values = courant[face, t].astype(F32).reshape(128, 128)
            for to in range(N_LON):
                courant_out[t, pl.ds(to * 32 + face * 8, 8)] = values[to * 8 : to * 8 + 8]

    def scatter(t):
        cells = jnp.transpose(note_in[...].astype(F32))
        cell_ids = lax.broadcasted_iota(jnp.int32, (512, 128), 0).astype(F32)
        total = jnp.zeros((512, 256), F32)
        for pair in range(4):
            hot, value = [], []
            for slot in (2 * pair, 2 * pair + 1):
                row = cells[t * 8 + slot : t * 8 + slot + 1]
                hot.append(jnp.where(cell_ids == row, 1.0, 0.0).astype(jnp.bfloat16))
                x = jac_in[t, pl.ds(slot, 128, stride=8)]
                high = x.astype(jnp.bfloat16)
                low = (x - high.astype(F32)).astype(jnp.bfloat16)
                value.append(jnp.concatenate([high, low], axis=1))
            total = total + jnp.dot(
                jnp.concatenate(hot, axis=1), jnp.concatenate(value, axis=0), preferred_element_type=F32
            )
        both = total[:, :128] + total[:, 128:]
        for row in range(4):
            by_entry = jnp.transpose(both[row * 128 : row * 128 + 128])
            for c in range(4):
                forcing[c, pl.ds(row, 32, stride=4)] = by_entry[c * 32 : c * 32 + 32]

    send_tiles(3, True)

    convert_courant(3)
    send_blocks(courant_out.at[3], courant_in.at[3], ks.at[1], kr.at[1])
    rates[...] = jnp.zeros_like(rates)
    rates[pl.ds(8, 124)] = mixing[...].astype(F32).reshape(124, 128)
    send_tiles(2, False)

    wait_bytes(note_in, nr)
    for i, row in enumerate((north, lat, south)):
        pltpu.make_async_copy(note_in.at[pl.ds(lon * N_LAT + row, 1)], shifts.at[pl.ds(i, 1)], sm.at[i]).start()
    wait_bytes(jac_in.at[3], jr.at[3])
    scatter(3)

    padded[...] = jnp.zeros_like(padded)
    for c in range(4):
        padded[c, pl.ds(8, 128)] = adj[c] + forcing[c]
        mid, above, below = padded[c, pl.ds(8, 128)], padded[c, pl.ds(12, 128)], padded[c, pl.ds(4, 128)]
        value = mid + rates[pl.ds(8, 128)] * (above - mid) - rates[pl.ds(4, 128)] * (mid - below)
        for to in range(N_LON):
            mixed[3, pl.ds(to * 32 + c * 8, 8)] = value[to * 8 : to * 8 + 8]
        padded[c, pl.ds(8, 128)] = value
        edges[0, pl.ds(c, 32, stride=4)] = padded[c, pl.ds(8, 32, stride=4)]
        edges[1, pl.ds(c, 32, stride=4)] = padded[c, pl.ds(11, 32, stride=4)]
    send_blocks(mixed.at[3], inbox.at[3], ps.at[0], pr.at[0])

    def send_edges(k, carry):
        target = lax.rem(lon + k, N_LON)
        to = group_of_lon(target)
        remote(
            edges.at[1, pl.ds(to * 8, 8)], halo.at[0, pl.ds(lon * 8, 8)], ps.at[1], pr.at[1], target, south
        ).start()
        remote(
            edges.at[0, pl.ds(to * 8, 8)], halo.at[1, pl.ds(lon * 8, 8)], ps.at[2], pr.at[2], target, north
        ).start()
        return carry

    lax.fori_loop(0, N_LON, send_edges, 0)

    def make_forcing(t):
        wait_bytes(jac_in.at[t], jr.at[t])
        scatter(t)
        for c in range(4):
            for to in range(N_LON):
                mixed[t, pl.ds(to * 32 + c * 8, 8)] = forcing[c, pl.ds(to * 8, 8)]
        send_blocks(mixed.at[t], inbox.at[t], fs.at[t], fr.at[t])

    make_forcing(2)

    pltpu.make_async_copy(rates.at[pl.ds(g * 8, 16)], rates_in.at[0, pl.ds(lon * 16, 16)], rr.at[0]).start()

    def send_rates(k, carry):
        target = lax.rem(lon + k, N_LON)
        to = group_of_lon(target)
        src = rates.at[pl.ds(to * 8, 16)]

        @pl.when(k > 0)
        def _():
            remote(src, rates_in.at[0, pl.ds(lon * 16, 16)], rs.at[0], rr.at[0], target, lat).start()

        remote(src, rates_in.at[1, pl.ds(lon * 16, 16)], rs.at[1], rr.at[1], target, south).start()
        remote(src, rates_in.at[2, pl.ds(lon * 16, 16)], rs.at[2], rr.at[2], target, north).start()
        return carry

    lax.fori_loop(0, N_LON, send_rates, 0)
    for t in range(3):
        convert_courant(t)
    pltpu.make_async_copy(
        courant_out.at[pl.ds(0, 3), pl.ds(g * 32, 32)], courant_in.at[pl.ds(0, 3), pl.ds(lon * 32, 32)], kr.at[0]
    ).start()

    def send_courant(to, target):
        remote(
            courant_out.at[pl.ds(0, 3), pl.ds(to * 32, 32)],
            courant_in.at[pl.ds(0, 3), pl.ds(lon * 32, 32)],
            ks.at[0], kr.at[0], target, lat,
        ).start()

    to_groups(send_courant)
    send_tiles(1, False)

    lane = lax.broadcasted_iota(jnp.int32, (16, 128), 1)
    flux[...] = jnp.zeros_like(flux)

    def loop_block(ref, at, first, stride):
        half = 8 * stride
        return jnp.concatenate(
            [ref[at, pl.ds(first, 8, stride=stride)], ref[at, pl.ds(first + half, 8, stride=stride)]], axis=0
        )

    def put_twice(i, value):
        twice[i, pl.ds(0, 16)] = value
        twice[i, pl.ds(16, 16)] = value

    def roll_rows(t):
        for row in range(6):
            i, j = (0, 3) if row == 0 else (2, 0) if row == 5 else (1, row - 1)
            shift = shifts[i, SHIFT_LANE + t * 4 + j]
            q, r = shift // 128, lax.rem(shift, 128)
            back = lax.rem(128 - r, 128)
            inside = lane < 128 - r

            def body(n, carry, row=row, q=q, back=back, inside=inside):
                i = row * 8 + n
                first = pltpu.roll(twice[i, pl.ds(q, 16)], back, 1)
                second = pltpu.roll(twice[i, pl.ds(q + 1, 16)], back, 1)
                value = jnp.where(inside, first, second)
                if row == 0:
                    value = jnp.where(lat == 0, 0.0, value)
                if row == 5:
                    value = jnp.where(lat == N_LAT - 1, 0.0, value)
                rolled[i] = value
                return carry

            lax.fori_loop(0, 8, body, 0, unroll=True)

    def transport(t, finish):
        def body(n, carry):
            l, row = n // 4, lax.rem(n, 4)
            faces = [
                jnp.concatenate(
                    [
                        courant_in[t, pl.ds(face * 8 + n, 8, stride=32)],
                        courant_in[t, pl.ds(256 + face * 8 + n, 8, stride=32)],
                    ],
                    axis=0,
                )
                for face in range(4)
            ]
            for c in range(4):
                i = (row + 1) * 8 + l * 4 + c
                x, up, down = rolled[i], rolled[i + 8], rolled[i - 8]
                e = pltpu.roll(x, 127, 1)
                east = jnp.where(lane == 127, pltpu.roll(e, 15, 0), e)
                w = pltpu.roll(x, 1, 1)
                west = jnp.where(lane == 0, pltpu.roll(w, 1, 0), w)
                value = (
                    x + faces[0] * (up - x) + faces[1] * (down - x) + faces[2] * (east - x) + faces[3] * (west - x)
                )
                finish(c, l, row, n, value)
            return carry

        lax.fori_loop(0, 8, body, 0, unroll=True)
        return None

    def add_forcing(t, e):
        def finish(c, l, row, n, value):
            at = pl.ds((c * 4 + row) * 16, 16)

            @pl.when(l == 0)
            def _():
                flux[at] = flux[at] + value

            state[e, row + 1, l + 1, c] = value + loop_block(inbox, t, c * 8 + n, 32)

        return finish

    def exchange(e):
        return [
            remote(state.at[e, pl.ds(1, 4), 2], state.at[e, pl.ds(1, 4), 0], es.at[e, 0], er.at[e, 0], lon_up, lat),
            remote(state.at[e, pl.ds(1, 4), 1], state.at[e, pl.ds(1, 4), 3], es.at[e, 1], er.at[e, 1], lon_down, lat),
            remote(state.at[e, 1, pl.ds(1, 2)], state.at[e, 5, pl.ds(1, 2)], es.at[e, 2], er.at[e, 2], lon, north),
            remote(state.at[e, 4, pl.ds(1, 2)], state.at[e, 0, pl.ds(1, 2)], es.at[e, 3], er.at[e, 3], lon, south),
            remote(state.at[e, 1, 2], state.at[e, 5, 0], es.at[e, 4], er.at[e, 4], lon_up, north),
            remote(state.at[e, 4, 2], state.at[e, 0, 0], es.at[e, 5], er.at[e, 5], lon_up, south),
            remote(state.at[e, 1, 1], state.at[e, 5, 3], es.at[e, 6], er.at[e, 6], lon_down, north),
            remote(state.at[e, 4, 1], state.at[e, 0, 3], es.at[e, 7], er.at[e, 7], lon_down, south),
        ]

    def mix_rows(e):
        for row in range(6):
            for l in range(2):
                low, high = rates_t[row, l], rates_t[row, l + 1]

                def body(c, carry, row=row, l=l, low=low, high=high):
                    mid = state[e, row, l + 1, c]
                    value = mid + high * (state[e, row, l + 2, c] - mid) - low * (mid - state[e, row, l, c])
                    put_twice(row * 8 + l * 4 + c, value)
                    return carry

                lax.fori_loop(0, 4, body, 0, unroll=True)

    wait_bytes(inbox.at[3], pr.at[0])
    wait_bytes(halo.at[0], pr.at[1])
    wait_bytes(halo.at[1], pr.at[2])
    for i in range(3):
        wait_bytes(note_in.at[pl.ds(0, 1)], sm.at[i])
    for l in range(2):
        for c in range(4):
            put_twice(l * 4 + c, loop_block(halo, 0, l * 4 + c, 8))
            put_twice(40 + l * 4 + c, loop_block(halo, 1, l * 4 + c, 8))
            for row in range(4):
                put_twice((row + 1) * 8 + l * 4 + c, loop_block(inbox, 3, c * 8 + l * 4 + row, 32))
    roll_rows(3)
    wait_bytes(courant_in.at[3], kr.at[1])
    wait_bytes(inbox.at[2], fr.at[2])
    transport(3, add_forcing(2, 0))
    moves = exchange(0)
    for move in moves:
        move.start()

    send_tiles(0, False)
    make_forcing(1)
    for i in range(3):
        wait_bytes(rates_in.at[i], rr.at[i])
    for level in range(3):
        for row in range(6):
            i, j = (1, 3) if row == 0 else (2, 0) if row == 5 else (0, row - 1)
            rates_t[row, level] = loop_block(rates_in, i, (level + 1) * 4 + j, 16)
    wait_bytes(courant_in.at[pl.ds(0, 3)], kr.at[0])

    for t in (2, 1):
        for move in moves:
            move.wait_recv()
        mix_rows(2 - t)
        roll_rows(t)
        wait_bytes(inbox.at[t - 1], fr.at[t - 1])
        transport(t, add_forcing(t - 1, 3 - t))
        for move in moves:
            move.wait_send()
        moves = exchange(3 - t)
        for move in moves:
            move.start()
        if t == 2:
            make_forcing(0)

    for move in moves:
        move.wait_recv()
    mix_rows(2)
    roll_rows(0)

    def finish(c, l, row, n, value):
        at = pl.ds((c * 4 + row) * 16, 16)

        @pl.when(l == 0)
        def _():
            flux[at] = flux[at] + value

        final[pl.ds((c * 8 + n) * 16, 16)] = value

    transport(0, finish)

    for d in range(N_LON):
        for c in range(4):
            final_out[d, c] = final[pl.ds(c * 128 + d, 8, stride=16)]
        flux_send[d] = flux[pl.ds(d, 16, stride=16)]
    mine = out.at[:, pl.ds(g * 8, 8)]
    pltpu.make_async_copy(final_out.at[lon], mine, orv).start()

    def send_out(k, carry):
        target = lax.rem(lon + k, N_LON)
        remote(final_out.at[target], mine, os, orv, target, lat).start()
        return carry

    lax.fori_loop(1, N_LON, send_out, 0)

    @pl.when(g == 0)
    def _():
        pltpu.make_async_copy(flux_send.at[lon], flux_out, xr).start()

        def send_flux(k, carry):
            target = lax.rem(lon + k, N_LON)
            remote(flux_send.at[target], flux_out, xs, xr, target, lat).start()
            return carry

        lax.fori_loop(1, N_LON, send_flux, 0)
        wait_bytes(flux_send.at[pl.ds(0, N_LON - 1)], xs)

    for move in moves:
        move.wait_send()
    for t in range(4):
        wait_bytes(jac_in.at[t, pl.ds(0, 8 * (N_DEV - 1))], js.at[t])
    wait_bytes(note_in.at[pl.ds(0, N_DEV - 1)], ns)
    wait_bytes(inbox.at[3, pl.ds(0, 480)], ps.at[0])
    wait_bytes(halo.at[0], ps.at[1])
    wait_bytes(halo.at[1], ps.at[2])
    for t in range(3):
        wait_bytes(inbox.at[t, pl.ds(0, 480)], fs.at[t])
    wait_bytes(courant_in.at[3, pl.ds(0, 480)], ks.at[1])
    wait_bytes(courant_in.at[pl.ds(0, 3), pl.ds(0, 480)], ks.at[0])
    wait_bytes(rates_in.at[0, pl.ds(0, 240)], rs.at[0])
    wait_bytes(rates_in.at[1], rs.at[1])
    wait_bytes(rates_in.at[2], rs.at[2])
    wait_bytes(final_out.at[pl.ds(0, N_LON - 1)], os)
    wait_bytes(out, orv)
    wait_bytes(flux_out, xr)


def shards(adjoint_end, face_courant, mixing, row_shift, tile_jac, tile_cell, tile_count):
    slots = lax.broadcasted_iota(jnp.int32, (4, N_DEV, 8), 2)
    cells = jnp.where(slots < tile_count[0][:, :, None], tile_cell[0], -1)
    cells = jnp.transpose(cells, (1, 0, 2)).reshape(N_DEV, 32)
    own_shift = jnp.broadcast_to(row_shift.reshape(1, 16), (N_DEV, 16))
    note = jnp.concatenate([cells, own_shift, jnp.zeros((N_DEV, 80), jnp.int32)], axis=1)
    dma = pltpu.SemaphoreType.DMA
    vmem = pltpu.VMEM
    whole = pl.BlockSpec(memory_space=pltpu.VMEM)
    out, flux = pl.pallas_call(
        kernel,
        out_shape=(
            jax.ShapeDtypeStruct((4, 128, 128), F32),
            jax.ShapeDtypeStruct((16, 128), F32),
        ),
        in_specs=[whole, whole, whole, pl.BlockSpec(memory_space=pl.ANY), whole],
        out_specs=(whole, whole),
        scratch_shapes=[
            vmem((4, 1024, 128), F32),
            vmem((128, 128), jnp.int32),
            pltpu.SMEM((3, 128), jnp.int32),
            vmem((4, 128, 128), F32),
            vmem((4, 144, 128), F32),
            vmem((144, 128), F32),
            vmem((4, 512, 128), F32),
            vmem((2, 128, 128), F32),
            vmem((4, 512, 128), F32),
            vmem((4, 512, 128), F32),
            vmem((2, 128, 128), F32),
            vmem((4, 512, 128), F32),
            vmem((3, 256, 128), F32),
            vmem((6, 3, 16, 128), F32),
            vmem((3, 6, 4, 4, 16, 128), F32),
            vmem((48, 32, 128), F32),
            vmem((48, 16, 128), F32),
            vmem((512, 128), F32),
            vmem((16, 4, 8, 128), F32),
            vmem((256, 128), F32),
            vmem((16, 16, 128), F32),
            dma((4,)), dma((4,)), dma, dma, dma((3,)), dma((3,)), dma((3,)), dma((3,)), dma((2,)), dma((2,)),
            dma((3,)), dma((3,)), dma((3, 8)), dma((3, 8)), dma, dma, dma, dma, dma((3,)),
        ],
        compiler_params=pltpu.CompilerParams(
            collective_id=0, has_side_effects=True, vmem_limit_bytes=48 * 1024 * 1024
        ),
    )(
        adjoint_end.reshape(4, 128, 128),
        face_courant,
        mixing,
        tile_jac.reshape(4, 1024, 128),
        note,
    )
    return out.reshape(4, 32, 4, 128), flux.reshape(4, 4, 128)


def solution(mesh):
    in_specs = (
        P(None, None, "lat", "lon"),
        P(None, None, None, "lat", "lon"),
        P(None, "lat", "lon"),
        P(None, "lat"),
        P(("lon", "lat"), None, None, None, None),
        P(("lon", "lat"), None, None, None),
        P(("lon", "lat"), None, None),
    )
    out_specs = (P(None, None, "lat", "lon"), P(None, "lat", "lon"))
    return jax.shard_map(shards, mesh=mesh, in_specs=in_specs, out_specs=out_specs, check_vma=False)
```

time: 509 us -> 106 us (0.21)
  waiting for transfers between devices: 278 us -> 0 us
  local copies, waits for them, and re-layouts: 115 us -> 6.65 us
  Pallas kernels: 0 us -> 96 us
  starting transfers between devices: 63.2 us -> 0 us
  other arithmetic: 29.5 us -> 0.74 us
  between operations: 14.3 us -> 0.66 us
    all_gather x4 -> x0, waiting for transfers between devices: 215 us -> none  [roll_rows(): whole_cycle = lax.all_gather(mixed, 'lon', axis=3, tiled=True)]
    pallas_call x0 -> x1, Pallas kernels: none -> 96 us  [shards(): pl.pallas_call(kernel, out_shape=(jax.ShapeDtypeStruct((4, 128, 128), F32...]
    transpose x4 -> x0, local copies, waits for them, and re-layouts: 60.5 us -> none  [take_row(): return lax.dynamic_slice_in_dim(row_block, offset, width, axis=2)]
    ppermute x16 -> x0, starting transfers between devices: 41.8 us -> none  [the longest x8 22.9 us: with_halo(): lax.ppermute(lax.slice_in_dim(block, 0, width, axis=dim), axis, backward)]
    all_to_all x3 -> x0, waiting for transfers between devices: 40.2 us -> none  [the longest x1 26.1 us: shards(): lax.all_to_all(tile_jac, ('lon', 'lat'), split_axis=2, concat_axis=0, til...]
    gather x8 -> x0, local copies, waits for them, and re-layouts: 32.9 us -> none  [take_row(): return lax.dynamic_slice_in_dim(row_block, offset, width, axis=2)]
    ppermute x16 -> x0, waiting for transfers between devices: 23.2 us -> none  [the longest x8 19.7 us: with_halo(): lax.ppermute(lax.slice_in_dim(block, 0, width, axis=dim), axis, backward)]
    all_to_all x3 -> x0, starting transfers between devices: 21.3 us -> none  [the longest x1 10.8 us: shards(): lax.all_to_all(tile_count, ('lon', 'lat'), split_axis=2, concat_axis=0, t...]
  transfers between devices with their start and end apart: 23 -> 0, of which waited for: 11 -> 0; matrix products, arithmetic and copies ran while one was open for 2% -> 0% of each run, Pallas kernels for 0% -> 0%
where the time goes in v1:
time: 106 us; the launch traced here: 104 us
  Pallas kernels  96 us (91%)
  local copies, waits for them, and re-layouts  6.65 us (6%)
    pallas_call x1, Pallas kernels, shards(): pl.pallas_call(kernel, out_shape=(jax.ShapeDtypeStruct((4, 128, 128), F32...  96 us
    unnamed x10, local copies, waits for them, and re-layouts  5.63 us

profile of v1, /device:TPU:3, one launch (start us, length us, event | category | flops | bytes accessed | tf_op | source)
XLA Modules:
  0.0 104.1 jit_solution(1451571655043644668)
XLA Ops:
  0.6 0.8 reshape.27
  1.4 0.1 pad.1.clone
  1.5 0.1 pad.2.clone
  1.5 0.7 fusion
  2.3 0.1 copy.10
  2.4 0.0 copy-start
  2.4 1.6 %copy-done = f32[1,4,128,8,128]{4,3,2,1,0:T(8,128)S(1)} copy-done((f32[1,4,128,8,128]{4,3,2,1,0:T(8,128)S(1)}, f32[1,4,128,8,128]{4,3,2,1,0:T(8,128)}, u32[]{:S(2)}) %copy-start) | copy-done | bytes 2097176
  4.0 0.0 copy-start.1
  4.0 1.0 copy-done.1
  5.0 0.0 copy-start.2
  5.0 0.9 copy-done.2
  6.0 0.0 copy-start.3
  6.0 0.8 copy-done.3
  6.7 96.0 %shard_map.86 = (f32[4,128,128]{2,1,0:T(8,128)S(1)}, f32[16,128]{1,0:T(8,128)S(1)}) custom-call(f32[4,128,128]{2,1,0:T(8,128)S(1)} %bitcast.14, bf16[4,4,32,4,128]{4,3,2,1,0:T(4,128)(2,1)S(1)} %copy-done.1, bf16[31,4,128]{2,1,0:T(4,128)(2,1)S(1)} %copy-done.3, f32[4,1024,128]{2,1,0:T(8,128)S(1)} %bitcast.13, s32[128,128]{1,0:T(8,128)S(1)} %add_add_fusion.note), custom_call_target="tpu_custom_call" | custom-call | tf_op jit(solution)/shard_map/pallas_call | solution.py:430
  102.8 0.7 copy.13
  103.5 0.6 copy.14
  (2 shorter events, 0.0 us)
Async XLA Ops:
  2.4 1.6 %copy-start = (f32[1,4,128,8,128]{4,3,2,1,0:T(8,128)S(1)}, f32[1,4,128,8,128]{4,3,2,1,0:T(8,128)}, u32[]{:S(2)}) copy-start(f32[1,4,128,8,128]{4,3,2,1,0:T(8,128)} %param.11) | copy-start | bytes 6291460
  4.0 1.0 %copy-start.1 = (bf16[4,4,32,4,128]{4,3,2,1,0:T(4,128)(2,1)S(1)}, bf16[4,4,32,4,128]{4,3,2,1,0:T(4,128)(2,1)}, u32[]{:S(2)}) copy-start(bf16[4,4,32,4,128]{4,3,2,1,0:T(4,128)(2,1)} %courant.1) | copy-start | bytes 1572868
  5.0 0.9 copy-start.2
  6.0 0.8 copy-start.3

commit v2 on v1

--- a/solution.py
+++ b/solution.py
@@ -13,6 +13,16 @@
 N_LAT = 8
 N_DEV = N_LON * N_LAT
 SHIFT_LANE = 32
+ORDER = {
+    "wait3": ("courant3", "send_cells", "turn2", "tiles2", "turn1", "send_rates", ),
+    "sent1": ("tiles1", "courant2", "courant1", "pass_rates", ),
+    "rolled3": ("wait_cells", "scatter2", ),
+    "sentE2": ("turn0", "tiles0", "courant0", "scatter1", "wait_rates", ),
+    "rolled2": (),
+    "sentE1": ("scatter0", ),
+    "rolled1": (),
+    "sentE0": (),
+}
 
 
 def lon_of_group(g):
@@ -44,11 +54,12 @@
 
 
 def kernel(
-    adj, courant, mixing, jac, note,
+    adj_hbm, courant_hbm, mixing_hbm, shift_hbm, jac, cell_hbm, count_hbm,
     out, flux_out,
+    adj, courant, mixing, own_shift, cell, count, note, raw, tiles_out, cells_out, cells_in, cells_t, values_t, force,
     jac_in, note_in, shifts, forcing, padded, rates, mixed, edges, courant_out,
     inbox, halo, courant_in, rates_in, rates_t, state, twice, rolled, final, final_out, flux, flux_send,
-    js, jr, ns, nr, ps, pr, fs, fr, ks, kr, rs, rr, es, er, os, orv, xs, xr, sm,
+    js, jr, ns, nr, ps, pr, ks, kr, rs, rr, es, er, os, orv, xs, xr, sm, ls, ws, wr, cs, cr, ts,
 ):
     lon, lat = lax.axis_index("lon"), lax.axis_index("lat")
     me = lon * N_LAT + lat
@@ -56,6 +67,20 @@
     north, south = lax.rem(lat + N_LAT - 1, N_LAT), lax.rem(lat + 1, N_LAT)
     lon_up, lon_down = lon_of_group(lax.rem(g + 1, N_LON)), lon_of_group(lax.rem(g + N_LON - 1, N_LON))
 
+    loads = [
+        pltpu.make_async_copy(src, dst, ls.at[i])
+        for i, (src, dst) in enumerate(
+            (
+                (cell_hbm, cell), (count_hbm, count), (shift_hbm, own_shift),
+                (courant_hbm, courant), (mixing_hbm, mixing), (adj_hbm, adj),
+            )
+        )
+    ]
+    for load in loads:
+        load.start()
+    for t in (2, 1, 0):
+        pltpu.make_async_copy(jac.at[t], raw.at[t], ts.at[t]).start()
+
     barrier = pltpu.get_barrier_semaphore()
 
     def peer(k):
@@ -66,6 +91,23 @@
         return carry
 
     lax.fori_loop(1, N_DEV, greet, 0)
+
+    for load in loads[:3]:
+        load.wait()
+    slots = lax.broadcasted_iota(jnp.int32, (8, 128), 0)
+    lines = [jnp.where(slots < count[t : t + 1], cell[t], -1) for t in range(4)]
+    lines += [jnp.full((1, 128), own_shift[i // 4, i % 4], jnp.int32) for i in range(16)]
+    by_owner = jnp.transpose(jnp.concatenate(lines + [jnp.zeros((80, 128), jnp.int32)], axis=0))
+    note[...] = by_owner
+
+    owner_lane = lax.broadcasted_iota(jnp.int32, (8, 128), 1) // 8
+    for t in range(3):
+        line = jnp.zeros((8, 128), jnp.int32)
+        for d in range(N_LON):
+            turned = pltpu.roll(by_owner[d * 8 : d * 8 + 8], (d * 8 - t * 8) % 128, 1)
+            line = jnp.where(owner_lane == d, turned, line)
+        cells_out[t] = line
+
     pl.semaphore_wait(barrier, N_DEV - 1)
 
     def send_tiles(t, notes):
@@ -83,6 +125,73 @@
             pltpu.make_async_copy(note.at[pl.ds(me, 1)], note_in.at[pl.ds(me, 1)], nr).start()
         pltpu.make_async_copy(jac.at[t, pl.ds(me * 8, 8)], jac_in.at[t, pl.ds(me * 8, 8)], jr.at[t]).start()
         lax.fori_loop(1, N_DEV, body, 0)
+
+    def turn_tiles(t):
+        pltpu.make_async_copy(jac.at[t], raw.at[t], ts.at[t]).wait()
+
+        def body(p, carry):
+            rows = [raw[t, pl.ds((d * N_LAT + p) * 8, 8)] for d in range(N_LON)]
+            entries = jnp.transpose(jnp.concatenate(rows, axis=0))
+            for c in range(4):
+                tiles_out[t, p, pl.ds(c, 32, stride=4)] = entries[c * 32 : c * 32 + 32]
+            return carry
+
+        lax.fori_loop(0, N_LAT, body, 0)
+
+    def send_turned(t):
+        def body(k, carry):
+            p_lon, p_lat = peer(k)
+            remote(
+                tiles_out.at[t, p_lat, pl.ds(group_of_lon(p_lon) * 8, 8)],
+                jac_in.at[t, pl.ds(me * 8, 8)],
+                js.at[t], jr.at[t], p_lon, p_lat,
+            ).start()
+            return carry
+
+        pltpu.make_async_copy(
+            tiles_out.at[t, lat, pl.ds(g * 8, 8)], jac_in.at[t, pl.ds(me * 8, 8)], jr.at[t]
+        ).start()
+        lax.fori_loop(1, N_DEV, body, 0)
+
+    def send_cells():
+        def body(k, carry):
+            p_lon, p_lat = peer(k)
+            remote(
+                cells_out.at[:, pl.ds(p_lat, 1)], cells_in.at[:, pl.ds(me, 1)], cs, cr, p_lon, p_lat
+            ).start()
+            return carry
+
+        pltpu.make_async_copy(cells_out.at[:, pl.ds(lat, 1)], cells_in.at[:, pl.ds(me, 1)], cr).start()
+        lax.fori_loop(1, N_DEV, body, 0)
+
+    def scatter_loop(t):
+        wait_bytes(jac_in.at[t], jr.at[t])
+        cells_t[...] = jnp.transpose(cells_in[t])
+        for e in range(8):
+            values_t[pl.ds(e * 128, 128)] = jnp.transpose(jac_in[t, pl.ds(e, 128, stride=8)])
+        columns = lax.broadcasted_iota(jnp.int32, (128, 128), 0)
+
+        def body(d, carry):
+            left, right = [], []
+            for slot in range(8):
+                place = cells_t[pl.ds(d * 8 + slot, 1)]
+                row, column = place >> 7, place & 127
+                value = values_t[pl.ds(d * 8 + slot, 8, stride=128)]
+                value = jnp.concatenate([jnp.where(row == r, value, 0.0) for r in range(4)], axis=0)
+                high = value.astype(jnp.bfloat16)
+                low = (value - high.astype(F32)).astype(jnp.bfloat16)
+                left.append(jnp.concatenate([high, low], axis=0))
+                right.append(jnp.where(columns == column, 1.0, 0.0).astype(jnp.bfloat16))
+            total = lax.dot_general(
+                jnp.concatenate(left, axis=1),
+                jnp.concatenate(right, axis=1),
+                (((1,), (1,)), ((), ())),
+                preferred_element_type=F32,
+            )
+            force[t, pl.ds(d, 32, stride=16)] = total[:32] + total[32:]
+            return carry
+
+        lax.fori_loop(0, N_LON, body, 0)
 
     def to_groups(send):
         def body(k, carry):
@@ -130,31 +239,79 @@
             for c in range(4):
                 forcing[c, pl.ds(row, 32, stride=4)] = by_entry[c * 32 : c * 32 + 32]
 
+    def send_rates():
+        loads[4].wait()
+        rates[...] = jnp.zeros_like(rates)
+        rates[pl.ds(8, 124)] = mixing[...].astype(F32).reshape(124, 128)
+        pltpu.make_async_copy(rates.at[pl.ds(8 + g * 8, 8)], rates_in.at[pl.ds(lon * 8, 8)], rr.at[0]).start()
+
+        def one(to, target):
+            remote(
+                rates.at[pl.ds(8 + to * 8, 8)], rates_in.at[pl.ds(lon * 8, 8)], rs.at[0], rr.at[0], target, lat
+            ).start()
+
+        to_groups(one)
+
+    rate_moves = [
+        remote(rates_t.at[pl.ds(1, 4), 2], rates_t.at[pl.ds(1, 4), 0], ws.at[0], wr.at[0], lon_up, lat),
+        remote(rates_t.at[1, pl.ds(1, 2)], rates_t.at[5, pl.ds(1, 2)], ws.at[1], wr.at[1], lon, north),
+        remote(rates_t.at[4, pl.ds(1, 2)], rates_t.at[0, pl.ds(1, 2)], ws.at[2], wr.at[2], lon, south),
+        remote(rates_t.at[1, 2], rates_t.at[5, 0], ws.at[3], wr.at[3], lon_up, north),
+        remote(rates_t.at[4, 2], rates_t.at[0, 0], ws.at[4], wr.at[4], lon_up, south),
+    ]
+
+    def pass_rates():
+        wait_bytes(rates_in, rr.at[0])
+        for l in range(2):
+            for row in range(4):
+                n = l * 4 + row
+                rates_t[row + 1, l + 1] = jnp.concatenate(
+                    [rates_in[pl.ds(n, 8, stride=8)], rates_in[pl.ds(64 + n, 8, stride=8)]], axis=0
+                )
+        for move in rate_moves:
+            move.start()
+
+    def wait_rates():
+        for move in rate_moves:
+            move.wait_recv()
+
+    def do(slot):
+        for name in ORDER[slot]:
+            what, t = name[:-1], int(name[-1]) if name[-1].isdigit() else None
+            if what == "courant":
+                convert_courant(t)
+                send_blocks(courant_out.at[t], courant_in.at[t], ks.at[t], kr.at[t])
+            elif what == "turn":
+                turn_tiles(t)
+            elif what == "tiles":
+                send_turned(t)
+            elif what == "scatter":
+                scatter_loop(t)
+            else:
+                {"send_rates": send_rates, "pass_rates": pass_rates, "wait_rates": wait_rates,
+                 "send_cells": send_cells, "wait_cells": lambda: wait_bytes(cells_in, cr)}[name]()
+
     send_tiles(3, True)
-
-    convert_courant(3)
-    send_blocks(courant_out.at[3], courant_in.at[3], ks.at[1], kr.at[1])
-    rates[...] = jnp.zeros_like(rates)
-    rates[pl.ds(8, 124)] = mixing[...].astype(F32).reshape(124, 128)
-    send_tiles(2, False)
-
+    loads[3].wait()
+    do("wait3")
     wait_bytes(note_in, nr)
     for i, row in enumerate((north, lat, south)):
         pltpu.make_async_copy(note_in.at[pl.ds(lon * N_LAT + row, 1)], shifts.at[pl.ds(i, 1)], sm.at[i]).start()
     wait_bytes(jac_in.at[3], jr.at[3])
     scatter(3)
 
+    loads[5].wait()
     padded[...] = jnp.zeros_like(padded)
     for c in range(4):
         padded[c, pl.ds(8, 128)] = adj[c] + forcing[c]
         mid, above, below = padded[c, pl.ds(8, 128)], padded[c, pl.ds(12, 128)], padded[c, pl.ds(4, 128)]
         value = mid + rates[pl.ds(8, 128)] * (above - mid) - rates[pl.ds(4, 128)] * (mid - below)
         for to in range(N_LON):
-            mixed[3, pl.ds(to * 32 + c * 8, 8)] = value[to * 8 : to * 8 + 8]
+            mixed[0, pl.ds(to * 32 + c * 8, 8)] = value[to * 8 : to * 8 + 8]
         padded[c, pl.ds(8, 128)] = value
         edges[0, pl.ds(c, 32, stride=4)] = padded[c, pl.ds(8, 32, stride=4)]
         edges[1, pl.ds(c, 32, stride=4)] = padded[c, pl.ds(11, 32, stride=4)]
-    send_blocks(mixed.at[3], inbox.at[3], ps.at[0], pr.at[0])
+    send_blocks(mixed.at[0], inbox.at[0], ps.at[0], pr.at[0])
 
     def send_edges(k, carry):
         target = lax.rem(lon + k, N_LON)
@@ -169,47 +326,7 @@
 
     lax.fori_loop(0, N_LON, send_edges, 0)
 
-    def make_forcing(t):
-        wait_bytes(jac_in.at[t], jr.at[t])
-        scatter(t)
-        for c in range(4):
-            for to in range(N_LON):
-                mixed[t, pl.ds(to * 32 + c * 8, 8)] = forcing[c, pl.ds(to * 8, 8)]
-        send_blocks(mixed.at[t], inbox.at[t], fs.at[t], fr.at[t])
-
-    make_forcing(2)
-
-    pltpu.make_async_copy(rates.at[pl.ds(g * 8, 16)], rates_in.at[0, pl.ds(lon * 16, 16)], rr.at[0]).start()
-
-    def send_rates(k, carry):
-        target = lax.rem(lon + k, N_LON)
-        to = group_of_lon(target)
-        src = rates.at[pl.ds(to * 8, 16)]
-
-        @pl.when(k > 0)
-        def _():
-            remote(src, rates_in.at[0, pl.ds(lon * 16, 16)], rs.at[0], rr.at[0], target, lat).start()
-
-        remote(src, rates_in.at[1, pl.ds(lon * 16, 16)], rs.at[1], rr.at[1], target, south).start()
-        remote(src, rates_in.at[2, pl.ds(lon * 16, 16)], rs.at[2], rr.at[2], target, north).start()
-        return carry
-
-    lax.fori_loop(0, N_LON, send_rates, 0)
-    for t in range(3):
-        convert_courant(t)
-    pltpu.make_async_copy(
-        courant_out.at[pl.ds(0, 3), pl.ds(g * 32, 32)], courant_in.at[pl.ds(0, 3), pl.ds(lon * 32, 32)], kr.at[0]
-    ).start()
-
-    def send_courant(to, target):
-        remote(
-            courant_out.at[pl.ds(0, 3), pl.ds(to * 32, 32)],
-            courant_in.at[pl.ds(0, 3), pl.ds(lon * 32, 32)],
-            ks.at[0], kr.at[0], target, lat,
-        ).start()
-
-    to_groups(send_courant)
-    send_tiles(1, False)
+    do("sent1")
 
     lane = lax.broadcasted_iota(jnp.int32, (16, 128), 1)
     flux[...] = jnp.zeros_like(flux)
@@ -283,21 +400,55 @@
             def _():
                 flux[at] = flux[at] + value
 
-            state[e, row + 1, l + 1, c] = value + loop_block(inbox, t, c * 8 + n, 32)
+            state[e, row + 1, l + 1, c] = value + force[t, pl.ds(((row * 2 + l) * 4 + c) * 16, 16)]
 
         return finish
 
     def exchange(e):
-        return [
-            remote(state.at[e, pl.ds(1, 4), 2], state.at[e, pl.ds(1, 4), 0], es.at[e, 0], er.at[e, 0], lon_up, lat),
-            remote(state.at[e, pl.ds(1, 4), 1], state.at[e, pl.ds(1, 4), 3], es.at[e, 1], er.at[e, 1], lon_down, lat),
-            remote(state.at[e, 1, pl.ds(1, 2)], state.at[e, 5, pl.ds(1, 2)], es.at[e, 2], er.at[e, 2], lon, north),
-            remote(state.at[e, 4, pl.ds(1, 2)], state.at[e, 0, pl.ds(1, 2)], es.at[e, 3], er.at[e, 3], lon, south),
-            remote(state.at[e, 1, 2], state.at[e, 5, 0], es.at[e, 4], er.at[e, 4], lon_up, north),
-            remote(state.at[e, 4, 2], state.at[e, 0, 0], es.at[e, 5], er.at[e, 5], lon_up, south),
-            remote(state.at[e, 1, 1], state.at[e, 5, 3], es.at[e, 6], er.at[e, 6], lon_down, north),
-            remote(state.at[e, 4, 1], state.at[e, 0, 3], es.at[e, 7], er.at[e, 7], lon_down, south),
-        ]
+        own, first, last = pl.ds(1, 4), 1, 4
+        moves = []
+        for dg, dl in ((1, 0), (-1, 0), (0, -1), (0, 1), (1, -1), (1, 1), (-1, -1), (-1, 1)):
+            rows = own if dl == 0 else first if dl < 0 else last
+            to_rows = own if dl == 0 else 5 if dl < 0 else 0
+            levels = pl.ds(1, 2) if dg == 0 else 2 if dg > 0 else 1
+            to_levels = pl.ds(1, 2) if dg == 0 else 0 if dg > 0 else 3
+            i = len(moves)
+            move = remote(
+                state.at[e, rows, levels], state.at[e, to_rows, to_levels], es.at[e, i], er.at[e, i],
+                lon if dg == 0 else lon_up if dg > 0 else lon_down,
+                lat if dl == 0 else north if dl < 0 else south,
+            )
+            sends, gets = [], []
+            if dg:
+                sends.append(g < N_LON - 1 if dg > 0 else g > 0)
+                gets.append(g > 0 if dg > 0 else g < N_LON - 1)
+            if dl:
+                sends.append(lat > 0 if dl < 0 else lat < N_LAT - 1)
+                gets.append(lat < N_LAT - 1 if dl < 0 else lat > 0)
+            moves.append((move, functools.reduce(jnp.logical_and, sends), functools.reduce(jnp.logical_and, gets)))
+        return moves
+
+    def start_moves(moves):
+        for move, sends, _ in moves:
+            pl.when(sends)(move.start)
+
+    def wait_moves(moves):
+        for move, _, gets in moves:
+            pl.when(gets)(move.wait_recv)
+
+    def end_moves(moves):
+        for move, sends, _ in moves:
+            pl.when(sends)(move.wait_send)
+
+    @pl.when(g == 0)
+    def _():
+        for e in range(3):
+            state[e, :, 0] = jnp.zeros_like(state[e, :, 0])
+
+    @pl.when(g == N_LON - 1)
+    def _():
+        for e in range(3):
+            state[e, :, 3] = jnp.zeros_like(state[e, :, 3])
 
     def mix_rows(e):
         for row in range(6):
@@ -312,7 +463,7 @@
 
                 lax.fori_loop(0, 4, body, 0, unroll=True)
 
-    wait_bytes(inbox.at[3], pr.at[0])
+    wait_bytes(inbox.at[0], pr.at[0])
     wait_bytes(halo.at[0], pr.at[1])
     wait_bytes(halo.at[1], pr.at[2])
     for i in range(3):
@@ -322,44 +473,32 @@
             put_twice(l * 4 + c, loop_block(halo, 0, l * 4 + c, 8))
             put_twice(40 + l * 4 + c, loop_block(halo, 1, l * 4 + c, 8))
             for row in range(4):
-                put_twice((row + 1) * 8 + l * 4 + c, loop_block(inbox, 3, c * 8 + l * 4 + row, 32))
+                put_twice((row + 1) * 8 + l * 4 + c, loop_block(inbox, 0, c * 8 + l * 4 + row, 32))
     roll_rows(3)
-    wait_bytes(courant_in.at[3], kr.at[1])
-    wait_bytes(inbox.at[2], fr.at[2])
+    wait_bytes(courant_in.at[3], kr.at[3])
+    do("rolled3")
     transport(3, add_forcing(2, 0))
     moves = exchange(0)
-    for move in moves:
-        move.start()
-
-    send_tiles(0, False)
-    make_forcing(1)
-    for i in range(3):
-        wait_bytes(rates_in.at[i], rr.at[i])
-    for level in range(3):
-        for row in range(6):
-            i, j = (1, 3) if row == 0 else (2, 0) if row == 5 else (0, row - 1)
-            rates_t[row, level] = loop_block(rates_in, i, (level + 1) * 4 + j, 16)
-    wait_bytes(courant_in.at[pl.ds(0, 3)], kr.at[0])
+    start_moves(moves)
+
+    do("sentE2")
 
     for t in (2, 1):
-        for move in moves:
-            move.wait_recv()
+        wait_moves(moves)
         mix_rows(2 - t)
         roll_rows(t)
-        wait_bytes(inbox.at[t - 1], fr.at[t - 1])
+        wait_bytes(courant_in.at[t], kr.at[t])
+        do(f"rolled{t}")
         transport(t, add_forcing(t - 1, 3 - t))
-        for move in moves:
-            move.wait_send()
+        end_moves(moves)
         moves = exchange(3 - t)
-        for move in moves:
-            move.start()
-        if t == 2:
-            make_forcing(0)
-
-    for move in moves:
-        move.wait_recv()
+        start_moves(moves)
+        do(f"sentE{t - 1}")
+
+    wait_moves(moves)
     mix_rows(2)
     roll_rows(0)
+    wait_bytes(courant_in.at[0], kr.at[0])
 
     def finish(c, l, row, n, value):
         at = pl.ds((c * 4 + row) * 16, 16)
@@ -398,32 +537,25 @@
         lax.fori_loop(1, N_LON, send_flux, 0)
         wait_bytes(flux_send.at[pl.ds(0, N_LON - 1)], xs)
 
-    for move in moves:
-        move.wait_send()
+    end_moves(moves)
     for t in range(4):
         wait_bytes(jac_in.at[t, pl.ds(0, 8 * (N_DEV - 1))], js.at[t])
     wait_bytes(note_in.at[pl.ds(0, N_DEV - 1)], ns)
-    wait_bytes(inbox.at[3, pl.ds(0, 480)], ps.at[0])
+    wait_bytes(cells_in.at[:, pl.ds(0, N_DEV - 1)], cs)
+    wait_bytes(inbox.at[0, pl.ds(0, 480)], ps.at[0])
     wait_bytes(halo.at[0], ps.at[1])
     wait_bytes(halo.at[1], ps.at[2])
-    for t in range(3):
-        wait_bytes(inbox.at[t, pl.ds(0, 480)], fs.at[t])
-    wait_bytes(courant_in.at[3, pl.ds(0, 480)], ks.at[1])
-    wait_bytes(courant_in.at[pl.ds(0, 3), pl.ds(0, 480)], ks.at[0])
-    wait_bytes(rates_in.at[0, pl.ds(0, 240)], rs.at[0])
-    wait_bytes(rates_in.at[1], rs.at[1])
-    wait_bytes(rates_in.at[2], rs.at[2])
+    for t in range(4):
+        wait_bytes(courant_in.at[t, pl.ds(0, 480)], ks.at[t])
+    wait_bytes(rates_in.at[pl.ds(0, 120)], rs.at[0])
+    for move in rate_moves:
+        move.wait_send()
     wait_bytes(final_out.at[pl.ds(0, N_LON - 1)], os)
     wait_bytes(out, orv)
     wait_bytes(flux_out, xr)
 
 
 def shards(adjoint_end, face_courant, mixing, row_shift, tile_jac, tile_cell, tile_count):
-    slots = lax.broadcasted_iota(jnp.int32, (4, N_DEV, 8), 2)
-    cells = jnp.where(slots < tile_count[0][:, :, None], tile_cell[0], -1)
-    cells = jnp.transpose(cells, (1, 0, 2)).reshape(N_DEV, 32)
-    own_shift = jnp.broadcast_to(row_shift.reshape(1, 16), (N_DEV, 16))
-    note = jnp.concatenate([cells, own_shift, jnp.zeros((N_DEV, 80), jnp.int32)], axis=1)
     dma = pltpu.SemaphoreType.DMA
     vmem = pltpu.VMEM
     whole = pl.BlockSpec(memory_space=pltpu.VMEM)
@@ -433,22 +565,36 @@
             jax.ShapeDtypeStruct((4, 128, 128), F32),
             jax.ShapeDtypeStruct((16, 128), F32),
         ),
-        in_specs=[whole, whole, whole, pl.BlockSpec(memory_space=pl.ANY), whole],
+        in_specs=[pl.BlockSpec(memory_space=pl.ANY)] * 7,
         out_specs=(whole, whole),
         scratch_shapes=[
+            vmem((4, 128, 128), F32),
+            vmem((4, 4, 32, 4, 128), jnp.bfloat16),
+            vmem((31, 4, 128), jnp.bfloat16),
+            pltpu.SMEM((4, 4), jnp.int32),
+            vmem((4, 8, 128), jnp.int32),
+            vmem((4, 128), jnp.int32),
+            vmem((128, 128), jnp.int32),
+            vmem((3, 1024, 128), F32),
+            vmem((3, 8, 128, 128), F32),
+            vmem((3, 8, 128), jnp.int32),
+            vmem((3, 128, 128), jnp.int32),
+            vmem((128, 128), jnp.int32),
+            vmem((1024, 128), F32),
+            vmem((3, 512, 128), F32),
             vmem((4, 1024, 128), F32),
             vmem((128, 128), jnp.int32),
             pltpu.SMEM((3, 128), jnp.int32),
             vmem((4, 128, 128), F32),
             vmem((4, 144, 128), F32),
             vmem((144, 128), F32),
-            vmem((4, 512, 128), F32),
+            vmem((1, 512, 128), F32),
             vmem((2, 128, 128), F32),
             vmem((4, 512, 128), F32),
-            vmem((4, 512, 128), F32),
+            vmem((1, 512, 128), F32),
             vmem((2, 128, 128), F32),
             vmem((4, 512, 128), F32),
-            vmem((3, 256, 128), F32),
+            vmem((128, 128), F32),
             vmem((6, 3, 16, 128), F32),
             vmem((3, 6, 4, 4, 16, 128), F32),
             vmem((48, 32, 128), F32),
@@ -457,18 +603,21 @@
             vmem((16, 4, 8, 128), F32),
             vmem((256, 128), F32),
             vmem((16, 16, 128), F32),
-            dma((4,)), dma((4,)), dma, dma, dma((3,)), dma((3,)), dma((3,)), dma((3,)), dma((2,)), dma((2,)),
-            dma((3,)), dma((3,)), dma((3, 8)), dma((3, 8)), dma, dma, dma, dma, dma((3,)),
+            dma((4,)), dma((4,)), dma, dma, dma((3,)), dma((3,)), dma((4,)), dma((4,)),
+            dma((1,)), dma((1,)), dma((3, 8)), dma((3, 8)), dma, dma, dma, dma, dma((3,)),
+            dma((6,)), dma((5,)), dma((5,)), dma, dma, dma((3,)),
         ],
         compiler_params=pltpu.CompilerParams(
-            collective_id=0, has_side_effects=True, vmem_limit_bytes=48 * 1024 * 1024
+            collective_id=0, has_side_effects=True, vmem_limit_bytes=60 * 1024 * 1024
         ),
     )(
         adjoint_end.reshape(4, 128, 128),
         face_courant,
         mixing,
+        row_shift,
         tile_jac.reshape(4, 1024, 128),
-        note,
+        jnp.transpose(tile_cell[0], (0, 2, 1)),
+        tile_count[0],
     )
     return out.reshape(4, 32, 4, 128), flux.reshape(4, 4, 128)
 

time: 106 us -> 84.8 us (0.80); the launches traced: 104 us -> 84.6 us
  Pallas kernels: 96 us -> 81 us
  local copies, waits for them, and re-layouts: 6.65 us -> 2.97 us
    pallas_call x1, Pallas kernels: 96 us -> 81 us  [shards(): pl.pallas_call(kernel, out_shape=(jax.ShapeDtypeStruct((4, 128, 128), F32...]
    unnamed x10 -> x2, local copies, waits for them, and re-layouts: 5.63 us -> 2.97 us
where the time goes in v2:
time: 84.8 us; the launch traced here: 84.6 us
  Pallas kernels  81 us (96%)
  local copies, waits for them, and re-layouts  2.97 us (4%)
    pallas_call x1, Pallas kernels, shards(): pl.pallas_call(kernel, out_shape=(jax.ShapeDtypeStruct((4, 128, 128), F32...  81 us
    unnamed x2, local copies, waits for them, and re-layouts  2.97 us

profile of v2, /device:TPU:3, one launch (start us, length us, event | category | flops | bytes accessed | tf_op | source)
XLA Modules:
  0.0 84.6 jit_solution(4388342243538374548)
XLA Ops:
  0.6 81.0 %shard_map.86 = (f32[4,128,128]{2,1,0:T(8,128)}, f32[16,128]{1,0:T(8,128)}) custom-call(f32[4,128,128]{2,1,0:T(8,128)} %bitcast.9, bf16[4,4,32,4,128]{4,3,2,1,0:T(4,128)(2,1)} %courant_hbm.1, bf16[31,4,128]{2,1,0:T(4,128)(2,1)} %mixing_hbm.1, s32[4,4]{1,0:T(4,128)} %shift_hbm.1, f32[4,1024,128]{2,1,0:T(8,128)} %bitcast.8, s32[4,8,128]{2,1,0:T(8,128)} %bitcast.11, ...), custom_call_target="tpu_custom_call" | custom-call | tf_op jit(solution)/shard_map/pallas_call | solution.py:562
  81.6 1.7 %copy.11 = f32[4,32,4,128]{3,2,1,0:T(4,128)} copy(f32[4,32,4,128]{3,2,1,0:T(4,128)} %bitcast.10) | data formatting | bytes 524288
  83.3 1.3 %copy.12 = f32[4,4,128]{2,1,0:T(4,128)} copy(f32[4,4,128]{2,1,0:T(4,128)} %bitcast.12) | data formatting | bytes 16384

commit v3 on v2

--- a/solution.py
+++ b/solution.py
@@ -14,16 +14,19 @@
 N_DEV = N_LON * N_LAT
 SHIFT_LANE = 32
 ORDER = {
-    "wait3": ("courant3", "send_cells", "turn2", "tiles2", "turn1", "send_rates", ),
-    "sent1": ("tiles1", "courant2", "courant1", "pass_rates", ),
+    "here": ("courant3", "send_rates", ),
+    "wait3": ("turn2", "tiles2", "turn1", ),
+    "sent1": ("send_cells", "tiles1", "pass_rates", "courant2", "turn0", "tiles0", ),
+    "got1": ("courant1", ),
     "rolled3": ("wait_cells", "scatter2", ),
-    "sentE2": ("turn0", "tiles0", "courant0", "scatter1", "wait_rates", ),
+    "sentE2": ("scatter1", "wait_rates", "return_rates", ),
+    "gotE2": (),
     "rolled2": (),
-    "sentE1": ("scatter0", ),
+    "sentE1": ("scatter0", "pass_edges", ),
+    "gotE1": (),
     "rolled1": (),
     "sentE0": (),
 }
-
 
 def lon_of_group(g):
     k = g // 2
@@ -56,10 +59,12 @@
 def kernel(
     adj_hbm, courant_hbm, mixing_hbm, shift_hbm, jac, cell_hbm, count_hbm,
     out, flux_out,
-    adj, courant, mixing, own_shift, cell, count, note, raw, tiles_out, cells_out, cells_in, cells_t, values_t, force,
+    adj, courant, mixing, own_shift, cell, count, note, raw, tiles_out, cells_out, cells_in, values_t, force,
     jac_in, note_in, shifts, forcing, padded, rates, mixed, edges, courant_out,
     inbox, halo, courant_in, rates_in, rates_t, state, twice, rolled, final, final_out, flux, flux_send,
-    js, jr, ns, nr, ps, pr, ks, kr, rs, rr, es, er, os, orv, xs, xr, sm, ls, ws, wr, cs, cr, ts,
+    rates0_out, rates0, rate_ends_out, rate_ends, rate_edge_out, rate_edge_in, rate_edge,
+    last, edge0_out, edge0, ends_out, ends, padded0, beside, flux_in,
+    js, jr, ns, nr, ps, pr, ks, kr, rs, rr, es, er, os, orv, xs, xr, sm, ls, ws, wr, cs, cr, ts, here, zs, zr,
 ):
     lon, lat = lax.axis_index("lon"), lax.axis_index("lat")
     me = lon * N_LAT + lat
@@ -78,37 +83,40 @@
     ]
     for load in loads:
         load.start()
-    for t in (2, 1, 0):
-        pltpu.make_async_copy(jac.at[t], raw.at[t], ts.at[t]).start()
 
     barrier = pltpu.get_barrier_semaphore()
 
     def peer(k):
+        k = lax.rem(k * 37, N_DEV)
         return lax.rem(lon + k // N_LAT, N_LON), lax.rem(lat + k % N_LAT, N_LAT)
 
-    def greet(k, carry):
-        pl.semaphore_signal(barrier, inc=1, device_id=peer(k), device_id_type=MESH)
+    def greet_group(k, carry):
+        pl.semaphore_signal(barrier, inc=1, device_id=(lax.rem(lon + k, N_LON), lat), device_id_type=MESH)
         return carry
 
-    lax.fori_loop(1, N_DEV, greet, 0)
+    def greet_column(k, carry):
+        pl.semaphore_signal(barrier, inc=1, device_id=(lon, lax.rem(lat + k, N_LAT)), device_id_type=MESH)
+        return carry
+
+    def greet_again(k, carry):
+        pl.semaphore_signal(here, inc=1, device_id=(lon, lax.rem(lat + k, N_LAT)), device_id_type=MESH)
+        return carry
+
+    lax.fori_loop(1, N_LAT, greet_column, 0)
+    lax.fori_loop(1, N_LON, greet_group, 0)
 
     for load in loads[:3]:
         load.wait()
     slots = lax.broadcasted_iota(jnp.int32, (8, 128), 0)
     lines = [jnp.where(slots < count[t : t + 1], cell[t], -1) for t in range(4)]
     lines += [jnp.full((1, 128), own_shift[i // 4, i % 4], jnp.int32) for i in range(16)]
-    by_owner = jnp.transpose(jnp.concatenate(lines + [jnp.zeros((80, 128), jnp.int32)], axis=0))
-    note[...] = by_owner
-
-    owner_lane = lax.broadcasted_iota(jnp.int32, (8, 128), 1) // 8
-    for t in range(3):
-        line = jnp.zeros((8, 128), jnp.int32)
-        for d in range(N_LON):
-            turned = pltpu.roll(by_owner[d * 8 : d * 8 + 8], (d * 8 - t * 8) % 128, 1)
-            line = jnp.where(owner_lane == d, turned, line)
-        cells_out[t] = line
-
-    pl.semaphore_wait(barrier, N_DEV - 1)
+    note[...] = jnp.transpose(jnp.concatenate(lines + [jnp.zeros((80, 128), jnp.int32)], axis=0))
+
+    for t in (2, 1, 0):
+        pltpu.make_async_copy(jac.at[t], raw.at[t], ts.at[t]).start()
+
+    pl.semaphore_wait(barrier, N_LON + N_LAT - 2)
+    lax.fori_loop(1, N_LAT, greet_again, 0)
 
     def send_tiles(t, notes):
         def body(k, carry):
@@ -154,19 +162,13 @@
         lax.fori_loop(1, N_DEV, body, 0)
 
     def send_cells():
-        def body(k, carry):
-            p_lon, p_lat = peer(k)
-            remote(
-                cells_out.at[:, pl.ds(p_lat, 1)], cells_in.at[:, pl.ds(me, 1)], cs, cr, p_lon, p_lat
-            ).start()
-            return carry
-
-        pltpu.make_async_copy(cells_out.at[:, pl.ds(lat, 1)], cells_in.at[:, pl.ds(me, 1)], cr).start()
-        lax.fori_loop(1, N_DEV, body, 0)
+        part = cells_out.at[pl.ds(0, 24)]
+        slot = cells_in.at[pl.ds(lon * 24, 24)]
+        pltpu.make_async_copy(part, slot, cr).start()
+        to_groups(lambda to, target: remote(part, slot, cs, cr, target, lat).start())
 
     def scatter_loop(t):
         wait_bytes(jac_in.at[t], jr.at[t])
-        cells_t[...] = jnp.transpose(cells_in[t])
         for e in range(8):
             values_t[pl.ds(e * 128, 128)] = jnp.transpose(jac_in[t, pl.ds(e, 128, stride=8)])
         columns = lax.broadcasted_iota(jnp.int32, (128, 128), 0)
@@ -174,7 +176,7 @@
         def body(d, carry):
             left, right = [], []
             for slot in range(8):
-                place = cells_t[pl.ds(d * 8 + slot, 1)]
+                place = cells_in[pl.ds(d * 24 + t * 8 + slot, 1)]
                 row, column = place >> 7, place & 127
                 value = values_t[pl.ds(d * 8 + slot, 8, stride=128)]
                 value = jnp.concatenate([jnp.where(row == r, value, 0.0) for r in range(4)], axis=0)
@@ -218,13 +220,12 @@
                 courant_out[t, pl.ds(to * 32 + face * 8, 8)] = values[to * 8 : to * 8 + 8]
 
     def scatter(t):
-        cells = jnp.transpose(note_in[...].astype(F32))
-        cell_ids = lax.broadcasted_iota(jnp.int32, (512, 128), 0).astype(F32)
+        cell_ids = lax.broadcasted_iota(jnp.int32, (512, 128), 0)
         total = jnp.zeros((512, 256), F32)
         for pair in range(4):
             hot, value = [], []
             for slot in (2 * pair, 2 * pair + 1):
-                row = cells[t * 8 + slot : t * 8 + slot + 1]
+                row = cells_out[t * 8 + slot : t * 8 + slot + 1]
                 hot.append(jnp.where(cell_ids == row, 1.0, 0.0).astype(jnp.bfloat16))
                 x = jac_in[t, pl.ds(slot, 128, stride=8)]
                 high = x.astype(jnp.bfloat16)
@@ -275,10 +276,78 @@
         for move in rate_moves:
             move.wait_recv()
 
+    def to_owners(x):
+        return jnp.where(lane < 32, pltpu.roll(x, 15, 0), pltpu.roll(x, 1, 0))
+
+    def return_rates():
+        column_ends = jnp.zeros((16, 128), F32)
+        for l in range(2):
+            for row in range(4):
+                n = l * 4 + row
+                value = rates_t[row + 1, l + 1]
+                twice[n, pl.ds(0, 16)] = value
+                twice[n, pl.ds(16, 16)] = value
+                value = take_rolled(twice, n, row_roll(0, row + 1))
+                final[pl.ds(n * 16, 16)] = value
+                same = lax.rem(lane, 8) == n
+                column_ends = jnp.where(same & (lane < 32), jnp.broadcast_to(value[:, :1], (16, 128)), column_ends)
+                column_ends = jnp.where(
+                    same & (lane >= 32), jnp.broadcast_to(value[:, 127:], (16, 128)), column_ends
+                )
+        rate_ends_out[...] = to_owners(column_ends)
+        for d in range(N_LON):
+            rates0_out[pl.ds(d * 8, 8)] = final[pl.ds(d, 8, stride=16)]
+        place = rates0.at[pl.ds(8 + g * 8, 8)]
+        pltpu.make_async_copy(rates0_out.at[pl.ds(lon * 8, 8)], place, zr.at[3]).start()
+        pltpu.make_async_copy(rate_ends_out.at[pl.ds(lon, 1)], rate_ends.at[pl.ds(g, 1)], zr.at[4]).start()
+
+        def one(to, target):
+            remote(rates0_out.at[pl.ds(target * 8, 8)], place, zs.at[3], zr.at[3], target, lat).start()
+            remote(
+                rate_ends_out.at[pl.ds(target, 1)], rate_ends.at[pl.ds(g, 1)], zs.at[4], zr.at[4], target, lat
+            ).start()
+
+        to_groups(one)
+
+    edge_moves = [
+        remote(rate_edge_out.at[0], rate_edge_in.at[1], zs.at[5], zr.at[5], lon, north),
+        remote(rate_edge_out.at[1], rate_edge_in.at[0], zs.at[6], zr.at[6], lon, south),
+    ]
+
+    def pass_edges():
+        wait_bytes(rates0.at[pl.ds(8, 128)], zr.at[3])
+        wait_bytes(rate_ends, zr.at[4])
+        rate_edge_out[0] = rates0[pl.ds(8, 32, stride=4)]
+        rate_edge_out[1] = rates0[pl.ds(11, 32, stride=4)]
+        for move in edge_moves:
+            move.start()
+
+    def take_edges():
+        for move in edge_moves:
+            move.wait()
+        for i in range(2):
+            for c in range(4):
+                rate_edge[i, pl.ds(8 + c, 32, stride=4)] = rate_edge_in[i]
+
+    none = jnp.zeros((8, 128), F32)
+    for i in range(2):
+        for at in (0, 136):
+            rate_edge[i, pl.ds(at, 8)] = none
+            edge0[i, pl.ds(at, 8)] = none
+    for at in (0, 136):
+        rates0[pl.ds(at, 8)] = none
+        for c in range(4):
+            last[c, pl.ds(at, 8)] = none
+            padded0[c, pl.ds(at, 8)] = none
+
+    lane = lax.broadcasted_iota(jnp.int32, (16, 128), 1)
+
     def do(slot):
         for name in ORDER[slot]:
             what, t = name[:-1], int(name[-1]) if name[-1].isdigit() else None
             if what == "courant":
+                if t == 3:
+                    loads[3].wait()
                 convert_courant(t)
                 send_blocks(courant_out.at[t], courant_in.at[t], ks.at[t], kr.at[t])
             elif what == "turn":
@@ -288,13 +357,16 @@
             elif what == "scatter":
                 scatter_loop(t)
             else:
-                {"send_rates": send_rates, "pass_rates": pass_rates, "wait_rates": wait_rates,
+                {"return_rates": return_rates, "pass_edges": pass_edges, "take_edges": take_edges, "send_rates": send_rates, "pass_rates": pass_rates, "wait_rates": wait_rates,
                  "send_cells": send_cells, "wait_cells": lambda: wait_bytes(cells_in, cr)}[name]()
 
+    do("here")
+    pl.semaphore_wait(here, N_LAT - 1)
+
     send_tiles(3, True)
-    loads[3].wait()
     do("wait3")
     wait_bytes(note_in, nr)
+    cells_out[...] = jnp.transpose(note_in[...])[:32]
     for i, row in enumerate((north, lat, south)):
         pltpu.make_async_copy(note_in.at[pl.ds(lon * N_LAT + row, 1)], shifts.at[pl.ds(i, 1)], sm.at[i]).start()
     wait_bytes(jac_in.at[3], jr.at[3])
@@ -328,7 +400,6 @@
 
     do("sent1")
 
-    lane = lax.broadcasted_iota(jnp.int32, (16, 128), 1)
     flux[...] = jnp.zeros_like(flux)
 
     def loop_block(ref, at, first, stride):
@@ -341,24 +412,30 @@
         twice[i, pl.ds(0, 16)] = value
         twice[i, pl.ds(16, 16)] = value
 
+    def row_roll(t, row):
+        i, j = (0, 3) if row == 0 else (2, 0) if row == 5 else (1, row - 1)
+        shift = shifts[i, SHIFT_LANE + t * 4 + j]
+        q, r = shift // 128, lax.rem(shift, 128)
+        return q, lax.rem(128 - r, 128), lane < 128 - r
+
+    def take_rolled(ref, i, roll):
+        q, back, inside = roll
+        first = pltpu.roll(ref[i, pl.ds(q, 16)], back, 1)
+        second = pltpu.roll(ref[i, pl.ds(q + 1, 16)], back, 1)
+        return jnp.where(inside, first, second)
+
     def roll_rows(t):
         for row in range(6):
-            i, j = (0, 3) if row == 0 else (2, 0) if row == 5 else (1, row - 1)
-            shift = shifts[i, SHIFT_LANE + t * 4 + j]
-            q, r = shift // 128, lax.rem(shift, 128)
-            back = lax.rem(128 - r, 128)
-            inside = lane < 128 - r
-
-            def body(n, carry, row=row, q=q, back=back, inside=inside):
+            roll = row_roll(t, row)
+
+            def body(n, carry, row=row, roll=roll):
                 i = row * 8 + n
-                first = pltpu.roll(twice[i, pl.ds(q, 16)], back, 1)
-                second = pltpu.roll(twice[i, pl.ds(q + 1, 16)], back, 1)
-                value = jnp.where(inside, first, second)
+                value = take_rolled(twice, i, roll)
                 if row == 0:
                     value = jnp.where(lat == 0, 0.0, value)
                 if row == 5:
                     value = jnp.where(lat == N_LAT - 1, 0.0, value)
-                rolled[i] = value
+                rolled[pl.ds(i * 16, 16)] = value
                 return carry
 
             lax.fori_loop(0, 8, body, 0, unroll=True)
@@ -378,7 +455,7 @@
             ]
             for c in range(4):
                 i = (row + 1) * 8 + l * 4 + c
-                x, up, down = rolled[i], rolled[i + 8], rolled[i - 8]
+                x, up, down = [rolled[pl.ds((i + 8 * k) * 16, 16)] for k in (0, 1, -1)]
                 e = pltpu.roll(x, 127, 1)
                 east = jnp.where(lane == 127, pltpu.roll(e, 15, 0), e)
                 w = pltpu.roll(x, 1, 1)
@@ -400,7 +477,11 @@
             def _():
                 flux[at] = flux[at] + value
 
-            state[e, row + 1, l + 1, c] = value + force[t, pl.ds(((row * 2 + l) * 4 + c) * 16, 16)]
+            value = value + force[t, pl.ds(((row * 2 + l) * 4 + c) * 16, 16)]
+            if t > 0:
+                state[e, row + 1, l + 1, c] = value
+            else:
+                put_twice((row + 1) * 8 + l * 4 + c, value)
 
         return finish
 
@@ -466,6 +547,7 @@
     wait_bytes(inbox.at[0], pr.at[0])
     wait_bytes(halo.at[0], pr.at[1])
     wait_bytes(halo.at[1], pr.at[2])
+    do("got1")
     for i in range(3):
         wait_bytes(note_in.at[pl.ds(0, 1)], sm.at[i])
     for l in range(2):
@@ -485,74 +567,146 @@
 
     for t in (2, 1):
         wait_moves(moves)
+        do(f"gotE{t}")
         mix_rows(2 - t)
         roll_rows(t)
         wait_bytes(courant_in.at[t], kr.at[t])
         do(f"rolled{t}")
         transport(t, add_forcing(t - 1, 3 - t))
         end_moves(moves)
-        moves = exchange(3 - t)
-        start_moves(moves)
-        do(f"sentE{t - 1}")
-
-    wait_moves(moves)
-    mix_rows(2)
-    roll_rows(0)
-    wait_bytes(courant_in.at[0], kr.at[0])
-
-    def finish(c, l, row, n, value):
-        at = pl.ds((c * 4 + row) * 16, 16)
-
-        @pl.when(l == 0)
-        def _():
-            flux[at] = flux[at] + value
-
-        final[pl.ds((c * 8 + n) * 16, 16)] = value
-
-    transport(0, finish)
-
+        if t == 2:
+            moves = exchange(1)
+            start_moves(moves)
+            do("sentE1")
+
+    column_ends = jnp.zeros((16, 128), F32)
+    for row in range(1, 5):
+        roll = row_roll(0, row)
+        for l in range(2):
+            for c in range(4):
+                i, n = row * 8 + l * 4 + c, c * 8 + l * 4 + row - 1
+                value = take_rolled(twice, i, roll)
+                rolled[pl.ds(i * 16, 16)] = value
+                final[pl.ds(n * 16, 16)] = value
+                column_ends = jnp.where(lane == n, pltpu.roll(value, n, 1), column_ends)
+                column_ends = jnp.where(lane == 32 + n, pltpu.roll(value, 33 + n, 1), column_ends)
+    ends_out[...] = to_owners(column_ends)
     for d in range(N_LON):
         for c in range(4):
             final_out[d, c] = final[pl.ds(c * 128 + d, 8, stride=16)]
+        edge0_out[0, pl.ds(d * 8, 8)] = rolled[pl.ds(128 + d, 8, stride=16)]
+        edge0_out[1, pl.ds(d * 8, 8)] = rolled[pl.ds(512 + d, 8, stride=16)]
         flux_send[d] = flux[pl.ds(d, 16, stride=16)]
-    mine = out.at[:, pl.ds(g * 8, 8)]
+    mine = last.at[:, pl.ds(8 + g * 8, 8)]
     pltpu.make_async_copy(final_out.at[lon], mine, orv).start()
-
-    def send_out(k, carry):
+    pltpu.make_async_copy(ends_out.at[pl.ds(lon, 1)], ends.at[pl.ds(g, 1)], zr.at[0]).start()
+
+    def send_last(k, carry):
         target = lax.rem(lon + k, N_LON)
-        remote(final_out.at[target], mine, os, orv, target, lat).start()
+
+        @pl.when(k > 0)
+        def _():
+            remote(final_out.at[target], mine, os, orv, target, lat).start()
+            remote(
+                ends_out.at[pl.ds(target, 1)], ends.at[pl.ds(g, 1)], zs.at[0], zr.at[0], target, lat
+            ).start()
+
+        part = pl.ds(target * 8, 8)
+        place = pl.ds(8 + g * 8, 8)
+        remote(edge0_out.at[0, part], edge0.at[1, place], zs.at[1], zr.at[1], target, north).start()
+        remote(edge0_out.at[1, part], edge0.at[0, place], zs.at[2], zr.at[2], target, south).start()
         return carry
 
-    lax.fori_loop(1, N_LON, send_out, 0)
+    lax.fori_loop(0, N_LON, send_last, 0)
 
     @pl.when(g == 0)
     def _():
-        pltpu.make_async_copy(flux_send.at[lon], flux_out, xr).start()
+        pltpu.make_async_copy(flux_send.at[lon], flux_in, xr).start()
 
         def send_flux(k, carry):
             target = lax.rem(lon + k, N_LON)
-            remote(flux_send.at[target], flux_out, xs, xr, target, lat).start()
+            remote(flux_send.at[target], flux_in, xs, xr, target, lat).start()
             return carry
 
         lax.fori_loop(1, N_LON, send_flux, 0)
         wait_bytes(flux_send.at[pl.ds(0, N_LON - 1)], xs)
 
-    end_moves(moves)
+    def mix_padded(ref, rate):
+        mid, above, below = ref[pl.ds(8, 128)], ref[pl.ds(12, 128)], ref[pl.ds(4, 128)]
+        return mid + rate[pl.ds(8, 128)] * (above - mid) - rate[pl.ds(4, 128)] * (mid - below)
+
+    take_edges()
+    wait_bytes(ends, zr.at[0])
+    upper = lax.rem(lane // 4, 2) == 1
+
+    def next_level(x):
+        return jnp.where(upper, pltpu.roll(pltpu.roll(x, 4, 1), 15, 0), pltpu.roll(x, 124, 1))
+
+    def level_before(x):
+        return jnp.where(upper, pltpu.roll(x, 4, 1), pltpu.roll(pltpu.roll(x, 124, 1), 1, 0))
+
+    x, rate = ends[...], rate_ends[...]
+    x = x + rate * (next_level(x) - x) - level_before(rate) * (x - level_before(x))
+    x = jnp.transpose(x)
+    for i in range(2):
+        wait_bytes(edge0.at[i, pl.ds(8, 128)], zr.at[1 if i == 1 else 2])
+        value = mix_padded(edge0.at[i], rate_edge.at[i])
+        value = jnp.where(lat == (0 if i == 0 else N_LAT - 1), 0.0, value)
+        padded0[0, pl.ds(8, 128)] = value
+        for c in range(4):
+            beside[i, c, pl.ds(3 * i, 32, stride=4)] = padded0[0, pl.ds(8 + c, 32, stride=4)]
+    wait_bytes(last.at[:, pl.ds(8, 128)], orv)
+    for c in range(4):
+        padded0[c, pl.ds(8, 128)] = mix_padded(last.at[c], rates0)
+    faces = [courant[face, 0].astype(F32).reshape(128, 128) for face in range(4)]
+    cell_row = lax.rem(lax.broadcasted_iota(jnp.int32, (128, 128), 0), 4)
+    cell_column = lax.broadcasted_iota(jnp.int32, (128, 128), 1)
+    wait_bytes(flux_in, xr)
+    for c in range(4):
+        mid = padded0[c, pl.ds(8, 128)]
+        up = jnp.where(cell_row == 3, beside[1, c], padded0[c, pl.ds(9, 128)])
+        down = jnp.where(cell_row == 0, beside[0, c], padded0[c, pl.ds(7, 128)])
+        right, left = [
+            jnp.concatenate(
+                [
+                    jnp.broadcast_to(x[first + c * 8 : first + c * 8 + 8, k : k + 1], (8, 128))
+                    for k in range(N_LON)
+                ],
+                axis=0,
+            )
+            for first in (0, 32)
+        ]
+        east = jnp.where(cell_column == 127, right, pltpu.roll(mid, 127, 1))
+        west = jnp.where(cell_column == 0, left, pltpu.roll(mid, 1, 1))
+        value = (
+            mid + faces[0] * (up - mid) + faces[1] * (down - mid) + faces[2] * (east - mid) + faces[3] * (west - mid)
+        )
+        out[c] = value
+        flux_out[pl.ds(c * 4, 4)] = flux_in[pl.ds(c * 4, 4)] + value[:4]
+
     for t in range(4):
         wait_bytes(jac_in.at[t, pl.ds(0, 8 * (N_DEV - 1))], js.at[t])
     wait_bytes(note_in.at[pl.ds(0, N_DEV - 1)], ns)
-    wait_bytes(cells_in.at[:, pl.ds(0, N_DEV - 1)], cs)
+    wait_bytes(cells_in.at[pl.ds(0, 24 * (N_LON - 1))], cs)
     wait_bytes(inbox.at[0, pl.ds(0, 480)], ps.at[0])
     wait_bytes(halo.at[0], ps.at[1])
     wait_bytes(halo.at[1], ps.at[2])
-    for t in range(4):
+    for t in range(1, 4):
         wait_bytes(courant_in.at[t, pl.ds(0, 480)], ks.at[t])
     wait_bytes(rates_in.at[pl.ds(0, 120)], rs.at[0])
     for move in rate_moves:
         move.wait_send()
     wait_bytes(final_out.at[pl.ds(0, N_LON - 1)], os)
-    wait_bytes(out, orv)
-    wait_bytes(flux_out, xr)
+    wait_bytes(ends_out.at[pl.ds(0, N_LON - 1)], zs.at[0])
+    wait_bytes(edge0_out.at[0], zs.at[1])
+    wait_bytes(edge0_out.at[1], zs.at[2])
+    wait_bytes(rates0_out.at[pl.ds(0, 120)], zs.at[3])
+    wait_bytes(rate_ends_out.at[pl.ds(0, N_LON - 1)], zs.at[4])
+
+
+def hand_over(field, flux, field_out, flux_out):
+    field_out[...] = field[...]
+    flux_out[...] = flux[...]
 
 
 def shards(adjoint_end, face_courant, mixing, row_shift, tile_jac, tile_cell, tile_count):
@@ -577,9 +731,8 @@
             vmem((128, 128), jnp.int32),
             vmem((3, 1024, 128), F32),
             vmem((3, 8, 128, 128), F32),
-            vmem((3, 8, 128), jnp.int32),
-            vmem((3, 128, 128), jnp.int32),
-            vmem((128, 128), jnp.int32),
+            vmem((32, 128), jnp.int32),
+            vmem((384, 128), jnp.int32),
             vmem((1024, 128), F32),
             vmem((3, 512, 128), F32),
             vmem((4, 1024, 128), F32),
@@ -598,14 +751,29 @@
             vmem((6, 3, 16, 128), F32),
             vmem((3, 6, 4, 4, 16, 128), F32),
             vmem((48, 32, 128), F32),
-            vmem((48, 16, 128), F32),
+            vmem((768, 128), F32),
             vmem((512, 128), F32),
             vmem((16, 4, 8, 128), F32),
             vmem((256, 128), F32),
             vmem((16, 16, 128), F32),
+            vmem((128, 128), F32),
+            vmem((144, 128), F32),
+            vmem((16, 128), F32),
+            vmem((16, 128), F32),
+            vmem((2, 32, 128), F32),
+            vmem((2, 32, 128), F32),
+            vmem((2, 144, 128), F32),
+            vmem((4, 144, 128), F32),
+            vmem((2, 128, 128), F32),
+            vmem((2, 144, 128), F32),
+            vmem((16, 128), F32),
+            vmem((16, 128), F32),
+            vmem((4, 144, 128), F32),
+            vmem((2, 4, 128, 128), F32),
+            vmem((16, 128), F32),
             dma((4,)), dma((4,)), dma, dma, dma((3,)), dma((3,)), dma((4,)), dma((4,)),
             dma((1,)), dma((1,)), dma((3, 8)), dma((3, 8)), dma, dma, dma, dma, dma((3,)),
-            dma((6,)), dma((5,)), dma((5,)), dma, dma, dma((3,)),
+            dma((6,)), dma((5,)), dma((5,)), dma, dma, dma((3,)), pltpu.SemaphoreType.REGULAR, dma((7,)), dma((7,)),
         ],
         compiler_params=pltpu.CompilerParams(
             collective_id=0, has_side_effects=True, vmem_limit_bytes=60 * 1024 * 1024
@@ -619,6 +787,12 @@
         jnp.transpose(tile_cell[0], (0, 2, 1)),
         tile_count[0],
     )
+    out, flux = pl.pallas_call(
+        hand_over,
+        out_shape=(jax.ShapeDtypeStruct((4, 128, 128), F32), jax.ShapeDtypeStruct((16, 128), F32)),
+        in_specs=[whole, whole],
+        out_specs=(whole, whole),
+    )(out, flux)
     return out.reshape(4, 32, 4, 128), flux.reshape(4, 4, 128)
 
 

time: 84.8 us -> 74.4 us (0.88)
  Pallas kernels: 81 us -> 73.6 us
  local copies, waits for them, and re-layouts: 2.97 us -> 0 us
    pallas_call x1, Pallas kernels: 81 us -> 71.9 us  [shards(): pl.pallas_call(kernel, out_shape=(jax.ShapeDtypeStruct((4, 128, 128), F32...]
    unnamed x2 -> x0, local copies, waits for them, and re-layouts: 2.97 us -> none
    pallas_call x0 -> x1, Pallas kernels: none -> 1.68 us  [shards(): pl.pallas_call(hand_over, out_shape=(jax.ShapeDtypeStruct((4, 128, 128),...]
where the time goes in v3:
time: 74.4 us; the launch traced here: 74.2 us
  Pallas kernels  73.6 us (99%)
    pallas_call x1, Pallas kernels, shards(): pl.pallas_call(kernel, out_shape=(jax.ShapeDtypeStruct((4, 128, 128), F32...  71.9 us
    pallas_call x1, Pallas kernels, shards(): pl.pallas_call(hand_over, out_shape=(jax.ShapeDtypeStruct((4, 128, 128),...  1.68 us

profile of v3, /device:TPU:3, one launch (start us, length us, event | category | flops | bytes accessed | tf_op | source)
XLA Modules:
  0.0 74.2 jit_solution(9838450808759318628)
XLA Ops:
  0.6 71.9 %shard_map.86 = (f32[4,128,128]{2,1,0:T(8,128)}, f32[16,128]{1,0:T(8,128)}) custom-call(f32[4,128,128]{2,1,0:T(8,128)} %bitcast.9, bf16[4,4,32,4,128]{4,3,2,1,0:T(4,128)(2,1)} %courant_hbm.1, bf16[31,4,128]{2,1,0:T(4,128)(2,1)} %mixing_hbm.1, s32[4,4]{1,0:T(4,128)} %shift_hbm.1, f32[4,1024,128]{2,1,0:T(8,128)} %bitcast.8, s32[4,8,128]{2,1,0:T(8,128)} %bitcast.10, ...), custom_call_target="tpu_custom_call" | custom-call | tf_op jit(solution)/shard_map/pallas_call | solution.py:716
  72.5 1.7 %shard_map.87 = (f32[4,128,128]{2,1,0:T(8,128)}, f32[16,128]{1,0:T(8,128)}) custom-call(f32[4,128,128]{2,1,0:T(8,128)} %get-tuple-element.6.field, f32[16,128]{1,0:T(8,128)} %get-tuple-element.7.flux), custom_call_target="tpu_custom_call" | custom-call | tf_op jit(solution)/shard_map/pallas_call | solution.py:790

commit v4 on v3

--- a/solution.py
+++ b/solution.py
@@ -14,12 +14,14 @@
 N_DEV = N_LON * N_LAT
 SHIFT_LANE = 32
 ORDER = {
+    "greeted": ("make_note", ),
     "here": ("courant3", "send_rates", ),
-    "wait3": ("turn2", "tiles2", "turn1", ),
-    "sent1": ("send_cells", "tiles1", "pass_rates", "courant2", "turn0", "tiles0", ),
-    "got1": ("courant1", ),
-    "rolled3": ("wait_cells", "scatter2", ),
-    "sentE2": ("scatter1", "wait_rates", "return_rates", ),
+    "wait3": ("send_notes", "turn2", "tiles2", "turn1", ),
+    "noted": ("send_cells", ),
+    "sent1": ("tiles1", "courant2", "pass_cells", "pass_rates", "turn0", "wait_cells", "scatter2", ),
+    "got1": (),
+    "rolled3": (),
+    "sentE2": ("tiles0", "courant1", "scatter1", "wait_rates", "return_rates", ),
     "gotE2": (),
     "rolled2": (),
     "sentE1": ("scatter0", "pass_edges", ),
@@ -105,32 +107,35 @@
     lax.fori_loop(1, N_LAT, greet_column, 0)
     lax.fori_loop(1, N_LON, greet_group, 0)
 
-    for load in loads[:3]:
-        load.wait()
-    slots = lax.broadcasted_iota(jnp.int32, (8, 128), 0)
-    lines = [jnp.where(slots < count[t : t + 1], cell[t], -1) for t in range(4)]
-    lines += [jnp.full((1, 128), own_shift[i // 4, i % 4], jnp.int32) for i in range(16)]
-    note[...] = jnp.transpose(jnp.concatenate(lines + [jnp.zeros((80, 128), jnp.int32)], axis=0))
-
-    for t in (2, 1, 0):
-        pltpu.make_async_copy(jac.at[t], raw.at[t], ts.at[t]).start()
-
-    pl.semaphore_wait(barrier, N_LON + N_LAT - 2)
-    lax.fori_loop(1, N_LAT, greet_again, 0)
-
-    def send_tiles(t, notes):
+
+    def make_note():
+        for load in loads[:3]:
+            load.wait()
+        slots = lax.broadcasted_iota(jnp.int32, (8, 128), 0)
+        lines = [jnp.where(slots < count[t : t + 1], cell[t], -1) for t in range(4)]
+        lines += [jnp.full((1, 128), own_shift[i // 4, i % 4], jnp.int32) for i in range(16)]
+        note[...] = jnp.transpose(jnp.concatenate(lines + [jnp.zeros((80, 128), jnp.int32)], axis=0))
+
+    def send_notes():
+        def body(k, carry):
+            p_lon, p_lat = peer(k)
+            remote(
+                note.at[pl.ds(p_lon * N_LAT + p_lat, 1)], note_in.at[pl.ds(me, 1)], ns, nr, p_lon, p_lat
+            ).start()
+            return carry
+
+        pltpu.make_async_copy(note.at[pl.ds(me, 1)], note_in.at[pl.ds(me, 1)], nr).start()
+        lax.fori_loop(1, N_DEV, body, 0)
+
+    def send_tiles(t):
         def body(k, carry):
             p_lon, p_lat = peer(k)
             owner = p_lon * N_LAT + p_lat
-            if notes:
-                remote(note.at[pl.ds(owner, 1)], note_in.at[pl.ds(me, 1)], ns, nr, p_lon, p_lat).start()
             remote(
                 jac.at[t, pl.ds(owner * 8, 8)], jac_in.at[t, pl.ds(me * 8, 8)], js.at[t], jr.at[t], p_lon, p_lat
             ).start()
             return carry
 
-        if notes:
-            pltpu.make_async_copy(note.at[pl.ds(me, 1)], note_in.at[pl.ds(me, 1)], nr).start()
         pltpu.make_async_copy(jac.at[t, pl.ds(me * 8, 8)], jac_in.at[t, pl.ds(me * 8, 8)], jr.at[t]).start()
         lax.fori_loop(1, N_DEV, body, 0)
 
@@ -161,11 +166,26 @@
         ).start()
         lax.fori_loop(1, N_DEV, body, 0)
 
+    core = lax.rem(lon, 2)
+
     def send_cells():
         part = cells_out.at[pl.ds(0, 24)]
-        slot = cells_in.at[pl.ds(lon * 24, 24)]
-        pltpu.make_async_copy(part, slot, cr).start()
-        to_groups(lambda to, target: remote(part, slot, cs, cr, target, lat).start())
+        slot = cells_in.at[pl.ds(core * 192 + lon // 2 * 24, 24)]
+        pltpu.make_async_copy(part, slot, cr.at[0]).start()
+
+        def body(k, carry):
+            remote(part, slot, cs.at[0], cr.at[0], lax.rem(lon + 2 * k, N_LON), lat).start()
+            return carry
+
+        lax.fori_loop(1, N_LON // 2, body, 0)
+
+    def core_cells():
+        half = cells_in.at[pl.ds(core * 192, 192)]
+        return remote(half, half, cs.at[1], cr.at[1], lon + 1 - 2 * core, lat)
+
+    def pass_cells():
+        wait_bytes(cells_in.at[pl.ds(core * 192, 192)], cr.at[0])
+        core_cells().start()
 
     def scatter_loop(t):
         wait_bytes(jac_in.at[t], jr.at[t])
@@ -176,7 +196,7 @@
         def body(d, carry):
             left, right = [], []
             for slot in range(8):
-                place = cells_in[pl.ds(d * 24 + t * 8 + slot, 1)]
+                place = cells_in[pl.ds(lax.rem(d, 2) * 192 + d // 2 * 24 + t * 8 + slot, 1)]
                 row, column = place >> 7, place & 127
                 value = values_t[pl.ds(d * 8 + slot, 8, stride=128)]
                 value = jnp.concatenate([jnp.where(row == r, value, 0.0) for r in range(4)], axis=0)
@@ -357,16 +377,24 @@
             elif what == "scatter":
                 scatter_loop(t)
             else:
-                {"return_rates": return_rates, "pass_edges": pass_edges, "take_edges": take_edges, "send_rates": send_rates, "pass_rates": pass_rates, "wait_rates": wait_rates,
-                 "send_cells": send_cells, "wait_cells": lambda: wait_bytes(cells_in, cr)}[name]()
-
+                {"make_note": make_note, "send_notes": send_notes, "return_rates": return_rates, "pass_edges": pass_edges, "take_edges": take_edges, "send_rates": send_rates, "pass_rates": pass_rates, "wait_rates": wait_rates,
+                 "send_cells": send_cells, "pass_cells": pass_cells, "wait_cells": lambda: core_cells().wait_recv()}[name]()
+
+    do("greeted")
+
+    for t in (2, 1, 0):
+        pltpu.make_async_copy(jac.at[t], raw.at[t], ts.at[t]).start()
+
+    pl.semaphore_wait(barrier, N_LON + N_LAT - 2)
+    lax.fori_loop(1, N_LAT, greet_again, 0)
     do("here")
     pl.semaphore_wait(here, N_LAT - 1)
 
-    send_tiles(3, True)
+    send_tiles(3)
     do("wait3")
     wait_bytes(note_in, nr)
     cells_out[...] = jnp.transpose(note_in[...])[:32]
+    do("noted")
     for i, row in enumerate((north, lat, south)):
         pltpu.make_async_copy(note_in.at[pl.ds(lon * N_LAT + row, 1)], shifts.at[pl.ds(i, 1)], sm.at[i]).start()
     wait_bytes(jac_in.at[3], jr.at[3])
@@ -687,7 +715,8 @@
     for t in range(4):
         wait_bytes(jac_in.at[t, pl.ds(0, 8 * (N_DEV - 1))], js.at[t])
     wait_bytes(note_in.at[pl.ds(0, N_DEV - 1)], ns)
-    wait_bytes(cells_in.at[pl.ds(0, 24 * (N_LON - 1))], cs)
+    wait_bytes(cells_in.at[pl.ds(0, 24 * 7)], cs.at[0])
+    core_cells().wait_send()
     wait_bytes(inbox.at[0, pl.ds(0, 480)], ps.at[0])
     wait_bytes(halo.at[0], ps.at[1])
     wait_bytes(halo.at[1], ps.at[2])
@@ -773,7 +802,7 @@
             vmem((16, 128), F32),
             dma((4,)), dma((4,)), dma, dma, dma((3,)), dma((3,)), dma((4,)), dma((4,)),
             dma((1,)), dma((1,)), dma((3, 8)), dma((3, 8)), dma, dma, dma, dma, dma((3,)),
-            dma((6,)), dma((5,)), dma((5,)), dma, dma, dma((3,)), pltpu.SemaphoreType.REGULAR, dma((7,)), dma((7,)),
+            dma((6,)), dma((5,)), dma((5,)), dma((2,)), dma((2,)), dma((3,)), pltpu.SemaphoreType.REGULAR, dma((7,)), dma((7,)),
         ],
         compiler_params=pltpu.CompilerParams(
             collective_id=0, has_side_effects=True, vmem_limit_bytes=60 * 1024 * 1024

time: 74.4 us -> 72.2 us (0.970); the launches traced: 74.2 us -> 71.1 us
  Pallas kernels: 73.6 us -> 70.5 us
    pallas_call x1, Pallas kernels: 71.9 us -> 68.8 us  [shards(): pl.pallas_call(kernel, out_shape=(jax.ShapeDtypeStruct((4, 128, 128), F32...]
where the time goes in v4:
time: 72.2 us; the launch traced here: 71.1 us
  Pallas kernels  70.5 us (98%)
    pallas_call x1, Pallas kernels, shards(): pl.pallas_call(kernel, out_shape=(jax.ShapeDtypeStruct((4, 128, 128), F32...  68.8 us
    pallas_call x1, Pallas kernels, shards(): pl.pallas_call(hand_over, out_shape=(jax.ShapeDtypeStruct((4, 128, 128),...  1.68 us

profile of v4, /device:TPU:3, one launch (start us, length us, event | category | flops | bytes accessed | tf_op | source)
XLA Modules:
  0.0 71.1 jit_solution(13996854040019082682)
XLA Ops:
  0.6 68.8 %shard_map.86 = (f32[4,128,128]{2,1,0:T(8,128)}, f32[16,128]{1,0:T(8,128)}) custom-call(f32[4,128,128]{2,1,0:T(8,128)} %bitcast.9, bf16[4,4,32,4,128]{4,3,2,1,0:T(4,128)(2,1)} %courant_hbm.1, bf16[31,4,128]{2,1,0:T(4,128)(2,1)} %mixing_hbm.1, s32[4,4]{1,0:T(4,128)} %shift_hbm.1, f32[4,1024,128]{2,1,0:T(8,128)} %bitcast.8, s32[4,8,128]{2,1,0:T(8,128)} %bitcast.10, ...), custom_call_target="tpu_custom_call" | custom-call | tf_op jit(solution)/shard_map/pallas_call | solution.py:745
  69.4 1.7 %shard_map.87 = (f32[4,128,128]{2,1,0:T(8,128)}, f32[16,128]{1,0:T(8,128)}) custom-call(f32[4,128,128]{2,1,0:T(8,128)} %get-tuple-element.6.field, f32[16,128]{1,0:T(8,128)} %get-tuple-element.7.flux), custom_call_target="tpu_custom_call" | custom-call | tf_op jit(solution)/shard_map/pallas_call | solution.py:819
